TPU v7x, 32 devices: a whole 2x2x4 slice. The times are simulated.
32 devices in a mesh: mem: 4 (over y, x), tile: 8 (over z, core).
Axes of the slice: x: 2, y: 2, z: 4, core: 2. Of those that a mesh axis runs over, the one named last changes fastest.
Arguments:
- perturbations: bfloat16 [20, 32, 24, 192], P('mem', None, 'tile'), may hold values from -6 to 6
- control: float32 [20, 32, 24, 192], P('mem', None, 'tile'), may hold values from -6 to 6
- filter_rate: float32 [24, 32], P('tile'), may hold values from 0.45 to 1, as said below
- lat_weight: int32 [48], P('tile'), may hold values from 0 to 256
- lon_weight: int32 [384], replicated, may hold values from 0 to 256
- wind_east: int32 [48, 384], P(None, 'tile'), may hold values from -480 to 480
- wind_north: int32 [48, 384], P(None, 'tile'), may hold values from -480 to 480
- obs_weight: float32 [32, 48, 384], P(None, None, 'tile'), may hold values from 1 to 16
Outputs:
- hessian_product: float32 [20, 32, 24, 192], P('mem', None, 'tile')
Inputs may be any that keep to these rules, and one draw needn't show every extreme that they name: `filter_rate`: every rate lies strictly below 1.
All inputs are finite; a program needn't handle non-finite values.
Results may differ from a plain program's by a relative error of at most 0.0003.
Values sent between devices are 32-bit elements; how exact they have to be, the bound alone decides.
A program may use at most 64 MiB of HBM per device.

v0:
```python
import jax
import jax.numpy as jnp
from jax import lax
from jax.sharding import PartitionSpec as P

STEPS = 3


LON_RATE = 0.8
HIGH = lax.Precision.HIGHEST


def with_halo(shard, sides, width):
    for axis, dim in sides:
        size, length = (lax.axis_size(axis), shard.shape[dim])
        up = [(i, (i + 1) % size) for i in range(size)]
        down = [(j, i) for i, j in up]
        last = lax.slice_in_dim(shard, length - width, length, axis=dim)
        leading = lax.slice_in_dim(shard, 0, width, axis=dim)
        before = lax.ppermute(last, axis, up)
        after = lax.ppermute(leading, axis, down)
        shard = jnp.concatenate([before, shard, after], axis=dim)
    return shard


def carried_in(part, axis, combine, identity, reverse):
    count = lax.axis_size(axis)
    place = lax.axis_index(axis)
    ahead = count - 1 - place if reverse else place
    gathered = jax.tree.map(lambda a: lax.all_gather(a, axis), part)
    state = jax.tree.map(lambda a, e: jnp.zeros_like(a) + jnp.asarray(e, a.dtype), part, identity)

    def one(turn, state):
        source = count - 1 - turn if reverse else turn
        return combine(
            state, jax.tree.map(lambda a: lax.dynamic_index_in_dim(a, source, 0, False), gathered)
        )

    return lax.fori_loop(0, ahead, one, state)


def shifted(block, axis, distance):
    devices = range(lax.axis_size(axis))
    route = [(i - distance, i) for i in devices if i - distance in devices]
    return lax.ppermute(block, axis, route)


def lon_table(col_count):
    across = jnp.arange(col_count)
    distance = across[None, :] - across[:, None]
    weight_scale = jnp.sqrt(jnp.float32(1.0 - LON_RATE * LON_RATE))
    powers = jnp.power(jnp.float32(LON_RATE), jnp.maximum(distance, 0).astype(jnp.float32))
    return jnp.where(distance >= 0, weight_scale * powers, jnp.float32(0.0))


def wind_terms(wind_east, wind_north):
    east_rate = wind_east.astype(jnp.float32) / 1024.0
    north_rate = wind_north.astype(jnp.float32) / 1024.0
    east_pos = jnp.maximum(east_rate, 0.0)
    east_neg = jnp.maximum(-east_rate, 0.0)
    north_pos = jnp.maximum(north_rate, 0.0)
    north_neg = jnp.maximum(-north_rate, 0.0)
    keep = 1.0 - east_pos - east_neg - north_pos - north_neg
    return (east_pos, east_neg, north_pos, north_neg, keep)


def compose(earlier, later):
    return (earlier[0] * later[0], later[0][None, :, None] * earlier[1] + later[1])


def advance(field_now, coeffs):
    east_pos, east_neg, north_pos, north_neg, keep = coeffs
    padded = with_halo(field_now, (("tile", 1),), 1)
    rows_pad = jnp.pad(field_now, ((0, 0), (0, 0), (1, 1)))
    result = keep * field_now + east_pos * padded[:, :-2, :] + east_neg * padded[:, 2:, :]
    return result + north_pos * rows_pad[:, :, :-2] + north_neg * rows_pad[:, :, 2:]


def retreat(field_now, coeffs):
    east_pos, east_neg, north_pos, north_neg, keep = coeffs
    padded = with_halo(field_now, (("tile", 1),), 1)
    from_east = east_pos[2:, :] * padded[:, 2:, :]
    from_west = east_neg[:-2, :] * padded[:, :-2, :]
    from_south = jnp.pad(north_pos[1:-1, :] * field_now, ((0, 0), (0, 0), (0, 1)))[:, :, 1:]
    from_north = jnp.pad(north_neg[1:-1, :] * field_now, ((0, 0), (0, 0), (1, 0)))[:, :, :-1]
    return keep[1:-1, :] * field_now + from_east + from_west + from_south + from_north


def local(
    perturbations, control, filter_rate, lat_weight, lon_weight, wind_east, wind_north, obs_weight
):
    member_count, level_count, coarse_rows, col_count = control.shape
    filter_table = lon_table(col_count)
    shrink = jnp.sqrt(1.0 - filter_rate * filter_rate)
    spread = 1.0 / jnp.sqrt(jnp.float32(member_count * lax.axis_size("mem") - 1))
    start_pair = (
        jnp.ones((level_count,), jnp.float32),
        jnp.zeros((member_count, level_count, col_count), jnp.float32),
    )
    smoothed = jnp.einsum("mvrc,cd->rmvd", control, filter_table, precision=HIGH)

    def forward_row(pair_now, inputs):
        gain_now, stretch = pair_now
        rate_row, shrink_row, row_vals = inputs
        gain_now = rate_row * gain_now
        stretch = rate_row[None, :, None] * stretch + shrink_row[None, :, None] * row_vals
        return ((gain_now, stretch), (gain_now, stretch))

    summary, (gains, stretches) = lax.scan(forward_row, start_pair, (filter_rate, shrink, smoothed))
    _, incoming = carried_in(summary, "tile", compose, start_pair, False)
    localized = gains[:, None, :, None] * incoming[None] + stretches
    partial_sum = spread * jnp.einsum(
        "mvrc,rmvc->vrc", perturbations.astype(jnp.float32), localized, precision=HIGH
    )
    increment = lax.psum(partial_sum, "mem")
    weight_here = obs_weight
    weight_here = jnp.swapaxes(weight_here, 1, 2)
    winds_turned = jnp.stack([jnp.transpose(wind_east), jnp.transpose(wind_north)])
    wind_halo = with_halo(winds_turned, (("tile", 1),), 1)
    halo_coeffs = wind_terms(wind_halo[0], wind_halo[1])
    inner_coeffs = tuple((term_item[1:-1, :] for term_item in halo_coeffs))
    level_here = increment.shape[0]
    tile_count = lax.axis_size("tile")
    band_cols = wind_east.shape[1]
    next_first = shifted(increment[:, :1, :], "tile", -1)
    window = band_cols // 2 + 2
    starts = jnp.arange(tile_count) * band_cols // 2
    cols_index = (starts[:, None] + jnp.arange(window)[None, :]) % col_count
    select = (jnp.arange(col_count)[:, None, None] == cols_index[None]).astype(jnp.float32)
    extended = jnp.concatenate([increment, next_first], axis=1)
    windows = jnp.einsum("vrc,cnk->vnrk", extended, select, precision=HIGH)
    arrived = lax.all_to_all(windows, "tile", split_axis=1, concat_axis=1, tiled=True)
    lat_every = lax.all_gather(lat_weight, "tile", axis=0, tiled=True)
    frac_every = (lat_every.astype(jnp.float32) / 256.0).reshape(1, tile_count, 2 * coarse_rows, 1)
    lower_rows = jnp.repeat(arrived[:, :, :-1, :], 2, axis=2)
    higher_rows = jnp.repeat(arrived[:, :, 1:, :], 2, axis=2)
    fine_window = (frac_every * lower_rows + (1.0 - frac_every) * higher_rows).reshape(
        level_here, tile_count * 2 * coarse_rows, window
    )
    first_col = lax.axis_index("tile") * band_cols
    fractions = (
        lax.dynamic_slice_in_dim(lon_weight, first_col, band_cols, 0).astype(jnp.float32) / 256.0
    )
    lower_local = (first_col + jnp.arange(band_cols)) // 2 - first_col // 2
    slots = jnp.arange(window)[:, None]
    band_interp = jnp.where(
        slots == lower_local[None, :], fractions[None, :], jnp.float32(0.0)
    ) + jnp.where(slots == lower_local[None, :] + 1, 1.0 - fractions[None, :], jnp.float32(0.0))
    field_now = jnp.einsum("vqk,kj->vjq", fine_window, band_interp, precision=HIGH)
    for step_index in range(STEPS):
        field_now = advance(field_now, inner_coeffs)
    field_now = weight_here * field_now
    for step_index in range(STEPS):
        field_now = retreat(field_now, halo_coeffs)
    rows_window = jnp.einsum("vjq,kj->vqk", field_now, band_interp, precision=HIGH).reshape(
        level_here, tile_count, 2 * coarse_rows, window
    )
    own_window = (
        (frac_every * rows_window)
        .reshape(level_here, tile_count, coarse_rows, 2, window)
        .sum(axis=3)
    )
    above_window = (
        ((1.0 - frac_every) * rows_window)
        .reshape(level_here, tile_count, coarse_rows, 2, window)
        .sum(axis=3)
    )
    extended_adjoint = jnp.pad(own_window, ((0, 0), (0, 0), (0, 1), (0, 0))) + jnp.pad(
        above_window, ((0, 0), (0, 0), (1, 0), (0, 0))
    )
    returned = lax.all_to_all(extended_adjoint, "tile", split_axis=1, concat_axis=1, tiled=True)
    column_sums = jnp.einsum("vnrk,cnk->vrc", returned, select, precision=HIGH)
    base_part = column_sums[:, :coarse_rows, :]
    edge_row = column_sums[:, coarse_rows:, :]
    carried = shifted(edge_row, "tile", 1)
    increment_adjoint = base_part + jnp.concatenate(
        [carried, jnp.zeros((level_here, coarse_rows - 1, col_count), jnp.float32)], axis=1
    )
    member_adjoint = spread * jnp.einsum(
        "mvrc,vrc->rmvc", perturbations.astype(jnp.float32), increment_adjoint, precision=HIGH
    )

    def backward_row(pair_now, inputs):
        gain_now, stretch = pair_now
        rate_row, row_vals = inputs
        outputs_here = (gain_now, stretch)
        gain_now = rate_row * gain_now
        stretch = rate_row[None, :, None] * (row_vals + stretch)
        return ((gain_now, stretch), outputs_here)

    summary_up, (gains_up, stretches_up) = lax.scan(
        backward_row, start_pair, (filter_rate, member_adjoint), reverse=True
    )
    _, incoming_up = carried_in(summary_up, "tile", compose, start_pair, True)
    summed = member_adjoint + gains_up[:, None, :, None] * incoming_up[None] + stretches_up
    scaled = summed * shrink[:, None, :, None]
    return control + jnp.einsum("rmvd,cd->mvrc", scaled, filter_table, precision=HIGH)


def solution(mesh):
    placed = (
        P("mem", None, "tile", None),
        P("mem", None, "tile", None),
        P("tile", None),
        P("tile"),
        P(),
        P(None, "tile"),
        P(None, "tile"),
        P(None, None, "tile"),
    )
    return jax.shard_map(
        local, mesh=mesh, in_specs=placed, out_specs=P("mem", None, "tile", None), check_vma=False
    )
```

profile of v0, /device:TPU:0, one launch (start us, length us, event | category | flops | bytes accessed | tf_op | source)
XLA Modules:
  0.0 210.3 jit_solution(2455262812264814685)
XLA Ops:
  6.5 0.8 subtract_sqrt_fusion
  7.3 1.6 convolution_bitcast_fusion.3
  9.0 0.6 while.66
  9.7 0.6 dynamic-slice
  11.2 18.1 %all-reduce.13 = f32[256]{0:T(256)S(1)} all-reduce(f32[256]{0:T(256)S(1)} %dynamic-update-slice.1), channel_id=2, replica_groups=mesh['mem'=4,'tile'=8] {'tile'}, use_global_device_ids=true, to_apply=%add.13 | all-reduce | flops 256 | bytes 2048
  29.3 17.0 %all-gather.1 = f32[40,32,192]{2,1,0:T(8,128)S(1)} all-gather(f32[5,32,192]{2,1,0:T(8,128)S(1)} %get-tuple-element.324), channel_id=3, replica_groups=mesh['mem'=4,'tile'=8] {'tile'}, dimensions={0}, use_global_device_ids=true | all-gather | bytes 1105920 | tf_op jit(solution)/shard_map/all_gather | solution.py:30
  46.4 0.9 copy-done
  47.5 0.7 broadcast_multiply_fusion.6
  48.6 3.2 %collective-permute-start.1 = (s32[2,1,48]{1,2,0:T(8,128)S(1)}, s32[2,1,48]{1,2,0:T(8,128)S(1)}, u32[]{:S(2)}, u32[]{:S(2)}) collective-permute-start(s32[2,1,48]{1,2,0:T(8,128)S(1)} %get-tuple-element.495), channel_id=1, source_target_pairs={{1,0},{2,1},{3,2},{4,3},{5,4},{6,5},{7,6},{0,7},{9,8},{10,9},{11,1... | collective-permute-start | bytes 1160 | tf_op jit(solution)/shard_map/ppermute | solution.py:21
  52.8 5.6 %all-reduce.12 = s32[48]{0:T(128)S(1)} all-reduce(s32[48]{0:T(128)S(1)} %dynamic-update-slice), channel_id=1, replica_groups=mesh['mem'=4,'tile'=8] {'tile'}, use_global_device_ids=true, to_apply=%add.12 | all-reduce | flops 48 | bytes 384
  58.4 0.8 broadcast_subtract_fusion.2
  59.1 30.0 %all-reduce.17.cloned.1.call-done = f32[32,3,192]{2,0,1:T(8,128)} async-done(((f32[32,3,192]{2,0,1:T(8,128)}), f32[32,3,192]{2,0,1:T(8,128)}) %all-reduce.17.cloned.1.call-update) | async-done | bytes 73744 | tf_op jit(solution)/shard_map/psum | solution.py:115
  89.1 0.8 slice.266
  89.9 1.3 collective-permute-start.2
  91.3 1.7 collective-permute-done.2
  93.0 1.3 convolution_bitcast_fusion.1
  94.6 0.9 reshape.184
  95.5 5.3 %all-to-all-start = ((f32[8,1,3328]{2,1,0:T(1,128)}), f32[8,1,3328]{2,1,0:T(1,128)S(1)}, u32[]{:S(2)}, u32[]{:S(2)}) async-start(f32[8,1,3328]{2,1,0:T(1,128)} %reshape.184), calls=%async_computation | async-start | bytes 212992 | tf_op jit(solution)/shard_map/all_to_all | solution.py:132
  100.8 6.4 %all-to-all-done = f32[8,1,3328]{2,1,0:T(1,128)S(1)} async-done(((f32[8,1,3328]{2,1,0:T(1,128)}), f32[8,1,3328]{2,1,0:T(1,128)S(1)}, u32[]{:S(2)}, u32[]{:S(2)}) %all-to-all-start) | async-done | bytes 106528 | tf_op jit(solution)/shard_map/all_to_all | solution.py:132
  107.7 0.9 reduce.2
  110.4 0.8 convolution_bitcast_fusion
  111.3 3.5 %collective-permute-start.4 = (f32[32,1,48]{2,1,0:T(1,128)S(1)}, f32[32,1,48]{2,1,0:T(1,128)S(1)}, u32[]{:S(2)}, u32[]{:S(2)}) collective-permute-start(f32[32,1,48]{2,1,0:T(1,128)S(1)} %get-tuple-element.487), channel_id=1, source_target_pairs={{1,0},{2,1},{3,2},{4,3},{5,4},{6,5},{7,6},{0,7},{9,8},{10,9},{11,1... | collective-permute-start | bytes 18440 | tf_op jit(solution)/shard_map/ppermute | solution.py:21
  115.3 0.9 collective-permute-done.3
  116.9 3.6 %collective-permute-start.6 = (f32[32,1,48]{2,1,0:T(1,128)S(1)}, f32[32,1,48]{2,1,0:T(1,128)S(1)}, u32[]{:S(2)}, u32[]{:S(2)}) collective-permute-start(f32[32,1,48]{2,1,0:T(1,128)S(1)} %get-tuple-element.485), channel_id=1, source_target_pairs={{1,0},{2,1},{3,2},{4,3},{5,4},{6,5},{7,6},{0,7},{9,8},{10,9},{11,1... | collective-permute-start | bytes 18440 | tf_op jit(solution)/shard_map/ppermute | solution.py:21
  120.6 1.3 collective-permute-done.5
  122.6 3.6 %collective-permute-start.8 = (f32[32,1,48]{2,1,0:T(1,128)S(1)}, f32[32,1,48]{2,1,0:T(1,128)S(1)}, u32[]{:S(2)}, u32[]{:S(2)}) collective-permute-start(f32[32,1,48]{2,1,0:T(1,128)S(1)} %get-tuple-element.483), channel_id=1, source_target_pairs={{1,0},{2,1},{3,2},{4,3},{5,4},{6,5},{7,6},{0,7},{9,8},{10,9},{11,1... | collective-permute-start | bytes 18440 | tf_op jit(solution)/shard_map/ppermute | solution.py:21
  126.6 0.9 collective-permute-done.7
  127.6 0.6 broadcast_multiply_fusion.5
  128.3 3.6 %collective-permute-start.9 = (f32[32,1,48]{2,1,0:T(1,128)S(1)}, f32[32,1,48]{2,1,0:T(1,128)S(1)}, u32[]{:S(2)}, u32[]{:S(2)}) collective-permute-start(f32[32,1,48]{2,1,0:T(1,128)S(1)} %get-tuple-element.480), channel_id=1, source_target_pairs={{1,0},{2,1},{3,2},{4,3},{5,4},{6,5},{7,6},{0,7},{9,8},{10,9},{11,1... | collective-permute-start | bytes 18440 | tf_op jit(solution)/shard_map/ppermute | solution.py:21
  131.9 1.3 collective-permute-done.10
  133.9 3.6 %collective-permute-start.11 = (f32[32,1,48]{2,1,0:T(1,128)S(1)}, f32[32,1,48]{2,1,0:T(1,128)S(1)}, u32[]{:S(2)}, u32[]{:S(2)}) collective-permute-start(f32[32,1,48]{2,1,0:T(1,128)S(1)} %get-tuple-element.478), channel_id=1, source_target_pairs={{1,0},{2,1},{3,2},{4,3},{5,4},{6,5},{7,6},{0,7},{9,8},{10,9},{11,1... | collective-permute-start | bytes 18440 | tf_op jit(solution)/shard_map/ppermute | solution.py:21
  137.6 1.4 collective-permute-done.11
  138.9 3.5 %collective-permute-done.12 = f32[32,1,48]{2,1,0:T(1,128)S(1)} collective-permute-done((f32[32,1,48]{2,1,0:T(1,128)S(1)}, f32[32,1,48]{2,1,0:T(1,128)S(1)}, u32[]{:S(2)}, u32[]{:S(2)}) %collective-permute-start.12) | collective-permute-done | bytes 6176 | tf_op jit(solution)/shard_map/ppermute | solution.py:20
  142.5 0.6 broadcast_multiply_fusion.3
  143.7 0.9 collective-permute-done.13
  144.6 3.8 %collective-permute-done.14 = f32[32,1,48]{2,1,0:T(1,128)S(1)} collective-permute-done((f32[32,1,48]{2,1,0:T(1,128)S(1)}, f32[32,1,48]{2,1,0:T(1,128)S(1)}, u32[]{:S(2)}, u32[]{:S(2)}) %collective-permute-start.14) | collective-permute-done | bytes 6176 | tf_op jit(solution)/shard_map/ppermute | solution.py:20
  148.3 1.1 fusion.13
  149.8 2.0 multiply_reduce_fusion.1
  152.3 8.8 %all_to_all.10 = f32[8,1,3328]{2,1,0:T(1,128)S(1)} all-to-all(f32[8,1,3328]{2,1,0:T(1,128)S(1)} %reshape.186), channel_id=1, replica_groups=mesh['mem'=4,'tile'=8] {'tile'}, dimensions={0} | all-to-all | bytes 212992 | tf_op jit(solution)/shard_map/all_to_all | solution.py:171
  161.1 0.9 reduce.3
  162.3 0.6 convolution_bitcast_fusion.4
  162.9 1.5 collective-permute-start.15
  164.5 0.8 collective-permute-done.15
  166.0 18.8 %all-gather.3 = f32[40,32,192]{2,1,0:T(8,128)S(1)} all-gather(f32[5,32,192]{2,1,0:T(8,128)S(1)} %get-tuple-element.329), channel_id=5, replica_groups=mesh['mem'=4,'tile'=8] {'tile'}, dimensions={0}, use_global_device_ids=true | all-gather | bytes 1105920 | tf_op jit(solution)/shard_map/all_gather | solution.py:30
  185.0 15.8 %all-reduce.14 = f32[256]{0:T(256)S(1)} all-reduce(f32[256]{0:T(256)S(1)} %dynamic-update-slice.2), channel_id=4, replica_groups=mesh['mem'=4,'tile'=8] {'tile'}, use_global_device_ids=true, to_apply=%add.14 | all-reduce | flops 256 | bytes 2048
  200.9 1.0 while.65
  201.9 0.7 fusion.8
  202.6 0.8 copy.57
  (137 shorter events, 11.7 us)
Async XLA Ops:
  6.5 2.5 %copy-start.5 = (f32[3,32]{1,0:T(4,128)S(1)}, f32[3,32]{1,0:T(4,128)}, u32[]{:S(2)}) copy-start(f32[3,32]{1,0:T(4,128)} %param.18) | copy-start | bytes 1156
  6.5 82.6 %all-reduce.17.cloned.1.call-start = ((), (), s32[]{:S(2)}) async-start(), calls=%async_computation.2 | async-start | bytes 196608 | tf_op jit(solution)/shard_map/psum | solution.py:115
  9.0 0.7 copy-start.7
  46.4 0.9 copy-start
  46.4 1.8 copy-start.3
  46.4 1.8 copy-start.4
  46.4 6.1 %copy-start.6 = (s32[6]{0:T(128)S(1)}, s32[6]{0:T(128)}, u32[]{:S(2)}) copy-start(s32[6]{0:T(128)} %param.19) | copy-start | bytes 76
  48.2 42.9 %collective-permute-start = (s32[2,1,48]{1,2,0:T(8,128)S(1)}, s32[2,1,48]{1,2,0:T(8,128)S(1)}, u32[]{:S(2)}, u32[]{:S(2)}) collective-permute-start(s32[2,1,48]{1,2,0:T(8,128)S(1)} %get-tuple-element.494), channel_id=1, source_target_pairs={{0,1},{1,2},{2,3},{3,4},{4,5},{5,6},{6,7},{7,0},{8,9},{9,10},{10,1... | collective-permute-start | bytes 1160 | tf_op jit(solution)/shard_map/ppermute | solution.py:20
  48.6 42.6 %collective-permute-start.1 = (s32[2,1,48]{1,2,0:T(8,128)S(1)}, s32[2,1,48]{1,2,0:T(8,128)S(1)}, u32[]{:S(2)}, u32[]{:S(2)}) collective-permute-start(s32[2,1,48]{1,2,0:T(8,128)S(1)} %get-tuple-element.495), channel_id=1, source_target_pairs={{1,0},{2,1},{3,2},{4,3},{5,4},{6,5},{7,6},{0,7},{9,8},{10,9},{11,1... | collective-permute-start | bytes 1160 | tf_op jit(solution)/shard_map/ppermute | solution.py:21
  89.9 3.1 %collective-permute-start.2 = (f32[32,1,192]{2,0,1:T(8,128)S(1)}, f32[32,1,192]{2,0,1:T(8,128)S(1)}, u32[]{:S(2)}, u32[]{:S(2)}) collective-permute-start(f32[32,1,192]{2,0,1:T(8,128)S(1)} %slice.266), channel_id=1, source_target_pairs={{1,0},{2,1},{3,2},{4,3},{5,4},{6,5},{7,6},{9,8},{10,9},{11,10},{12... | collective-permute-start | bytes 73736 | tf_op jit(solution)/shard_map/ppermute | solution.py:45
  95.5 11.7 %all-to-all-start = ((f32[8,1,3328]{2,1,0:T(1,128)}), f32[8,1,3328]{2,1,0:T(1,128)S(1)}, u32[]{:S(2)}, u32[]{:S(2)}) async-start(f32[8,1,3328]{2,1,0:T(1,128)} %reshape.184), calls=%async_computation | async-start | bytes 212992 | tf_op jit(solution)/shard_map/all_to_all | solution.py:132
  111.2 5.0 %collective-permute-start.3 = (f32[32,1,48]{2,1,0:T(1,128)S(1)}, f32[32,1,48]{2,1,0:T(1,128)S(1)}, u32[]{:S(2)}, u32[]{:S(2)}) collective-permute-start(f32[32,1,48]{2,1,0:T(1,128)S(1)} %get-tuple-element.486), channel_id=1, source_target_pairs={{0,1},{1,2},{2,3},{3,4},{4,5},{5,6},{6,7},{7,0},{8,9},{9,10},{10,1... | collective-permute-start | bytes 18440 | tf_op jit(solution)/shard_map/ppermute | solution.py:20
  111.3 5.0 %collective-permute-start.4 = (f32[32,1,48]{2,1,0:T(1,128)S(1)}, f32[32,1,48]{2,1,0:T(1,128)S(1)}, u32[]{:S(2)}, u32[]{:S(2)}) collective-permute-start(f32[32,1,48]{2,1,0:T(1,128)S(1)} %get-tuple-element.487), channel_id=1, source_target_pairs={{1,0},{2,1},{3,2},{4,3},{5,4},{6,5},{7,6},{0,7},{9,8},{10,9},{11,1... | collective-permute-start | bytes 18440 | tf_op jit(solution)/shard_map/ppermute | solution.py:21
  116.8 9.4 %copy-start.2 = (f32[32,48,48]{2,1,0:T(8,128)S(1)}, f32[32,48,48]{2,1,0:T(8,128)}, u32[]{:S(2)}) copy-start(f32[32,48,48]{2,1,0:T(8,128)} %param.23) | copy-start | bytes 884740
  116.8 5.0 %collective-permute-start.5 = (f32[32,1,48]{2,1,0:T(1,128)S(1)}, f32[32,1,48]{2,1,0:T(1,128)S(1)}, u32[]{:S(2)}, u32[]{:S(2)}) collective-permute-start(f32[32,1,48]{2,1,0:T(1,128)S(1)} %get-tuple-element.484), channel_id=1, source_target_pairs={{0,1},{1,2},{2,3},{3,4},{4,5},{5,6},{6,7},{7,0},{8,9},{9,10},{10,1... | collective-permute-start | bytes 18440 | tf_op jit(solution)/shard_map/ppermute | solution.py:20
  116.9 5.0 %collective-permute-start.6 = (f32[32,1,48]{2,1,0:T(1,128)S(1)}, f32[32,1,48]{2,1,0:T(1,128)S(1)}, u32[]{:S(2)}, u32[]{:S(2)}) collective-permute-start(f32[32,1,48]{2,1,0:T(1,128)S(1)} %get-tuple-element.485), channel_id=1, source_target_pairs={{1,0},{2,1},{3,2},{4,3},{5,4},{6,5},{7,6},{0,7},{9,8},{10,9},{11,1... | collective-permute-start | bytes 18440 | tf_op jit(solution)/shard_map/ppermute | solution.py:21
  122.5 5.0 %collective-permute-start.7 = (f32[32,1,48]{2,1,0:T(1,128)S(1)}, f32[32,1,48]{2,1,0:T(1,128)S(1)}, u32[]{:S(2)}, u32[]{:S(2)}) collective-permute-start(f32[32,1,48]{2,1,0:T(1,128)S(1)} %get-tuple-element.482), channel_id=1, source_target_pairs={{0,1},{1,2},{2,3},{3,4},{4,5},{5,6},{6,7},{7,0},{8,9},{9,10},{10,1... | collective-permute-start | bytes 18440 | tf_op jit(solution)/shard_map/ppermute | solution.py:20
  122.6 5.0 %collective-permute-start.8 = (f32[32,1,48]{2,1,0:T(1,128)S(1)}, f32[32,1,48]{2,1,0:T(1,128)S(1)}, u32[]{:S(2)}, u32[]{:S(2)}) collective-permute-start(f32[32,1,48]{2,1,0:T(1,128)S(1)} %get-tuple-element.483), channel_id=1, source_target_pairs={{1,0},{2,1},{3,2},{4,3},{5,4},{6,5},{7,6},{0,7},{9,8},{10,9},{11,1... | collective-permute-start | bytes 18440 | tf_op jit(solution)/shard_map/ppermute | solution.py:21
  128.2 5.0 %collective-permute-start.10 = (f32[32,1,48]{2,1,0:T(1,128)S(1)}, f32[32,1,48]{2,1,0:T(1,128)S(1)}, u32[]{:S(2)}, u32[]{:S(2)}) collective-permute-start(f32[32,1,48]{2,1,0:T(1,128)S(1)} %get-tuple-element.481), channel_id=1, source_target_pairs={{0,1},{1,2},{2,3},{3,4},{4,5},{5,6},{6,7},{7,0},{8,9},{9,10},{10,1... | collective-permute-start | bytes 18440 | tf_op jit(solution)/shard_map/ppermute | solution.py:20
  128.3 5.0 %collective-permute-start.9 = (f32[32,1,48]{2,1,0:T(1,128)S(1)}, f32[32,1,48]{2,1,0:T(1,128)S(1)}, u32[]{:S(2)}, u32[]{:S(2)}) collective-permute-start(f32[32,1,48]{2,1,0:T(1,128)S(1)} %get-tuple-element.480), channel_id=1, source_target_pairs={{1,0},{2,1},{3,2},{4,3},{5,4},{6,5},{7,6},{0,7},{9,8},{10,9},{11,1... | collective-permute-start | bytes 18440 | tf_op jit(solution)/shard_map/ppermute | solution.py:21
  133.9 5.0 %collective-permute-start.11 = (f32[32,1,48]{2,1,0:T(1,128)S(1)}, f32[32,1,48]{2,1,0:T(1,128)S(1)}, u32[]{:S(2)}, u32[]{:S(2)}) collective-permute-start(f32[32,1,48]{2,1,0:T(1,128)S(1)} %get-tuple-element.478), channel_id=1, source_target_pairs={{1,0},{2,1},{3,2},{4,3},{5,4},{6,5},{7,6},{0,7},{9,8},{10,9},{11,1... | collective-permute-start | bytes 18440 | tf_op jit(solution)/shard_map/ppermute | solution.py:21
  137.5 5.0 %collective-permute-start.12 = (f32[32,1,48]{2,1,0:T(1,128)S(1)}, f32[32,1,48]{2,1,0:T(1,128)S(1)}, u32[]{:S(2)}, u32[]{:S(2)}) collective-permute-start(f32[32,1,48]{2,1,0:T(1,128)S(1)} %get-tuple-element.479), channel_id=1, source_target_pairs={{0,1},{1,2},{2,3},{3,4},{4,5},{5,6},{6,7},{7,0},{8,9},{9,10},{10,1... | collective-permute-start | bytes 18440 | tf_op jit(solution)/shard_map/ppermute | solution.py:20
  143.1 1.5 collective-permute-start.13
  143.1 5.2 %collective-permute-start.14 = (f32[32,1,48]{2,1,0:T(1,128)S(1)}, f32[32,1,48]{2,1,0:T(1,128)S(1)}, u32[]{:S(2)}, u32[]{:S(2)}) collective-permute-start(f32[32,1,48]{2,1,0:T(1,128)S(1)} %get-tuple-element.477), channel_id=1, source_target_pairs={{0,1},{1,2},{2,3},{3,4},{4,5},{5,6},{6,7},{7,0},{8,9},{9,10},{10,1... | collective-permute-start | bytes 18440 | tf_op jit(solution)/shard_map/ppermute | solution.py:20
  162.9 2.4 %collective-permute-start.15 = (f32[32,1,192]{2,0,1:T(8,128)S(1)}, f32[32,1,192]{2,0,1:T(8,128)S(1)}, u32[]{:S(2)}, u32[]{:S(2)}) collective-permute-start(f32[32,1,192]{2,0,1:T(8,128)S(1)} %slice.288), channel_id=1, source_target_pairs={{0,1},{1,2},{2,3},{3,4},{4,5},{5,6},{6,7},{8,9},{9,10},{10,11},{11... | collective-permute-start | bytes 73736 | tf_op jit(solution)/shard_map/ppermute | solution.py:45
  200.9 1.0 copy-start.1
Sparse Core Ops, SparseCore 0:
  48.3 40.8 all-reduce.16
where the time goes:
time: 211 us; the launch traced here: 210 us
  blocking collectives  84.1 us (40%)
  waiting for transfers between devices  53.2 us (25%)
  starting transfers between devices  30.3 us (14%)
  between operations  15.2 us (7%)
  other arithmetic  11.3 us (5%)
  local copies, waits for them, and re-layouts  9.56 us (5%)
  matrix products  6.19 us (3%)
    unnamed x3, blocking collectives  39.4 us
    all_gather x2, blocking collectives, carried_in(): gathered = jax.tree.map(lambda a: lax.all_gather(a, axis), part)  35.9 us
    psum x1, waiting for transfers between devices, local(): increment = lax.psum(partial_sum, 'mem')  30 us
    ppermute x7, starting transfers between devices, with_halo(): after = lax.ppermute(leading, axis, down)  21.1 us
    ppermute x7, waiting for transfers between devices, with_halo(): before = lax.ppermute(last, axis, up)  11.7 us
    all_to_all x1, blocking collectives, local(): lax.all_to_all(extended_adjoint, 'tile', split_axis=1, concat_axis=1, til...  8.84 us
    all_to_all x1, waiting for transfers between devices, local(): lax.all_to_all(windows, 'tile', split_axis=1, concat_axis=1, tiled=True)  6.44 us
    all_to_all x1, starting transfers between devices, local(): lax.all_to_all(windows, 'tile', split_axis=1, concat_axis=1, tiled=True)  5.29 us
  transfers between devices with their start and end apart: 18, of which 15 were waited for; matrix products, arithmetic and copies ran while one was open for 2% of the time, Pallas kernels for 0%

commit v1 on v0

--- a/solution.py
+++ b/solution.py
@@ -1,9 +1,16 @@
+import functools
+
 import jax
 import jax.numpy as jnp
+import ml_dtypes
+import numpy as np
 from jax import lax
+from jax.experimental import pallas as pl
+from jax.experimental.pallas import tpu as pltpu
 from jax.sharding import PartitionSpec as P
 
 STEPS = 3
+MESH = pl.DeviceIdType.MESH
 
 
 LON_RATE = 0.8
@@ -196,6 +203,334 @@
     scaled = summed * shrink[:, None, :, None]
     return control + jnp.einsum("rmvd,cd->mvrc", scaled, filter_table, precision=HIGH)
 
+def split(x):
+    high = x.astype(jnp.bfloat16)
+    return high, (x - high.astype(jnp.float32)).astype(jnp.bfloat16)
+
+
+def product(a, b, turned):
+    dims = (((1,), (1 if turned else 0,)), ((), ()))
+
+    def one(left, right):
+        return lax.dot_general(left, right, dims, preferred_element_type=jnp.float32)
+
+    total = None
+    for i, left in enumerate(a):
+        for j, right in enumerate(b):
+            if i + j < 2:
+                term = one(left, right)
+                total = term if total is None else total + term
+    return total
+
+
+def hessian_kernel(
+    tiles, mems, rows_fine, spread,
+    ctl, prt, rates, small, winds, obs, lon, table_high, table_low,
+    out,
+    smalls, winds_all, obs_all, send_a, got_a, send_b, got_b, parts, parts_got,
+    levels_out, levels_in, adj_out, adj_in, own_adj, adj_all, send_c, got_c, send_d, got_d,
+    tile_send, tile_recv, mem_send, mem_recv,
+):
+    rows, members, levels, cols = ctl.shape
+    t = lax.axis_index("tile")
+    m = lax.axis_index("mem")
+    f32 = jnp.float32
+    started = []
+
+    barrier = pltpu.get_barrier_semaphore()
+    for d in range(1, tiles):
+        pl.semaphore_signal(
+            barrier, inc=1, device_id={"tile": lax.rem(t + d, tiles)}, device_id_type=MESH
+        )
+    for d in range(1, mems):
+        pl.semaphore_signal(
+            barrier, inc=1, device_id={"mem": lax.rem(m + d, mems)}, device_id_type=MESH
+        )
+
+    def spread_out(kind, axis, source, target):
+        size, me = (tiles, t) if axis == "tile" else (mems, m)
+        sends, recvs = (tile_send, tile_recv) if axis == "tile" else (mem_send, mem_recv)
+        copies = []
+        for d in range(1, size):
+            dest = lax.rem(me + d, size)
+            copy = pltpu.make_async_remote_copy(
+                src_ref=source(dest),
+                dst_ref=target.at[me],
+                send_sem=sends.at[kind, d],
+                recv_sem=recvs.at[kind, d],
+                device_id={axis: dest},
+                device_id_type=MESH,
+            )
+            copy.start()
+            copies.append(copy)
+        target[me] = source(me)[...]
+        started.extend(copies)
+        return copies
+
+    def arrive(copies):
+        for copy in copies:
+            copy.wait_recv()
+
+    rate = [rates[:, r : r + 1] for r in range(rows)]
+    shrink = [jnp.sqrt(1.0 - a * a) for a in rate]
+
+    def store_pieces(target, value):
+        for lane_part in range(-(-cols // 128)):
+            low = 128 * lane_part
+            width = min(128, cols - low)
+            for group in range(levels // 8):
+                piece = lane_part * (levels // 8) + group
+                block = value[:, 8 * group : 8 * group + 8, low : low + width]
+                if width < 128:
+                    block = jnp.concatenate(
+                        [block, jnp.zeros((members, 8, 128 - width), f32)], axis=2
+                    )
+                target[piece] = block
+
+    def load_pieces(source):
+        groups = levels // 8
+        lanes = []
+        for lane_part in range(-(-cols // 128)):
+            width = min(128, cols - 128 * lane_part)
+            blocks = [source[lane_part * groups + g] for g in range(groups)]
+            lanes.append(jnp.concatenate(blocks, axis=1)[:, :, :width])
+        return jnp.concatenate(lanes, axis=2)
+
+    local_rows = []
+    state = None
+    for r in range(rows):
+        term = shrink[r] * ctl[r]
+        state = term if r == 0 else rate[r] * state + term
+        local_rows.append(state)
+    store_pieces(send_a, state)
+
+    pl.semaphore_wait(barrier, tiles - 1 + mems - 1)
+    small_copies = spread_out(0, "tile", lambda dest: small, smalls)
+    carry_copies = spread_out(1, "tile", lambda dest: send_a.at[dest], got_a)
+    wind_copies = spread_out(2, "tile", lambda dest: winds, winds_all)
+    obs_copies = spread_out(3, "tile", lambda dest: obs.at[dest], obs_all)
+
+    table = (table_high[...], table_low[...])
+
+    def smooth(x, turned):
+        flat = x.reshape(members * levels, cols)
+        return product(split(flat), table, turned).reshape(members, levels, cols)
+
+    smooth_rows = [smooth(x, False) for x in local_rows]
+
+    arrive(small_copies)
+    group = lax.rem(t, levels // 8)
+    lane = lax.broadcasted_iota(jnp.int32, (8, 128), 1)
+    sub = lax.broadcasted_iota(jnp.int32, (8, 128), 0)
+    gain_mask = lane == sub + 8 * group
+    gains = []
+    for s in range(tiles):
+        row = smalls[s, 1:2, :]
+        gains.append(jnp.sum(jnp.where(gain_mask, row, 0.0), axis=1, keepdims=True))
+    arrive(carry_copies)
+    state = jnp.zeros((members, 8, 128), f32)
+    for s in range(tiles):
+        send_b[s] = state
+        state = gains[s] * state + got_a[s]
+    back_copies = spread_out(4, "tile", lambda dest: send_b.at[dest], got_b)
+
+    levels_out[...] = jnp.zeros_like(levels_out)
+    interp_row = lax.broadcasted_iota(jnp.int32, (lon.shape[0], cols), 0) // 2
+    interp_col = lax.broadcasted_iota(jnp.int32, (lon.shape[0], cols), 1)
+    west = lon[...]
+    interp = jnp.where(interp_col == interp_row, west, 0.0) + jnp.where(
+        interp_col == lax.rem(interp_row + 1, cols), 1.0 - west, 0.0
+    )
+    interp = (interp.astype(jnp.bfloat16),)
+    lat = smalls[0, 0:1, :]
+    for s in range(1, tiles):
+        lat = lat + smalls[s, 0:1, :]
+    slot = lax.broadcasted_iota(jnp.int32, (8 * tiles, 128), 0)
+    fine_row = lax.broadcasted_iota(jnp.int32, (8 * tiles, 128), 1) // 2
+    coarse = jnp.where(slot % 8 < rows, slot // 8 * rows + slot % 8, -2)
+    inside = fine_row < rows * tiles
+    lat_table = jnp.where((fine_row == coarse) & inside, lat, 0.0) + jnp.where(
+        (fine_row + 1 == coarse) & inside, 1.0 - lat, 0.0
+    )
+    lat_table = (lat_table.astype(jnp.bfloat16),)
+
+    arrive(back_copies)
+    carried = smooth(load_pieces(got_b), False)
+    gain = None
+    group_levels = levels // mems
+    for r in range(rows):
+        gain = rate[r] if r == 0 else gain * rate[r]
+        localized = gain * carried + smooth_rows[r]
+        partial = spread * jnp.sum(prt[r] * localized, axis=0)
+        for i in range(mems):
+            parts[i, r] = partial[i * group_levels : (i + 1) * group_levels]
+    part_copies = spread_out(0, "mem", lambda dest: parts.at[dest], parts_got)
+
+    arrive(wind_copies)
+    arrive(obs_copies)
+    count = lon.shape[0]
+    both = winds_all[...].reshape(count, 128)
+    keep_lane = lax.broadcasted_iota(jnp.int32, (count, 128), 1) < rows_fine
+    east = jnp.where(keep_lane, both, 0.0)
+    north = jnp.where(keep_lane, pltpu.roll(both, 64, 1), 0.0)
+    east_pos = jnp.maximum(east, 0.0)
+    east_neg = jnp.maximum(-east, 0.0)
+    north_pos = jnp.maximum(north, 0.0)
+    north_neg = jnp.maximum(-north, 0.0)
+    keep = 1.0 - east_pos - east_neg - north_pos - north_neg
+    arrive(part_copies)
+    for r in range(rows):
+        total = parts_got[0, r]
+        for i in range(1, mems):
+            total = total + parts_got[i, r]
+        for level in range(group_levels):
+            levels_out[level, r : r + 1, :] = total[level : level + 1, :]
+    level_copies = spread_out(5, "tile", lambda dest: levels_out.at[dest], levels_in)
+    arrive(level_copies)
+
+    increment = levels_in[...].reshape(8 * tiles, cols)
+    by_lon = product(interp, split(increment), True)
+    g = product(split(by_lon), lat_table, False)
+    for _ in range(STEPS):
+        g = (
+            keep * g
+            + east_pos * pltpu.roll(g, 1, 0)
+            + east_neg * pltpu.roll(g, count - 1, 0)
+            + north_pos * pltpu.roll(g, 1, 1)
+            + north_neg * pltpu.roll(g, 127, 1)
+        )
+    g = obs_all[...].reshape(count, 128) * g
+    for _ in range(STEPS):
+        g = (
+            keep * g
+            + pltpu.roll(east_pos * g, count - 1, 0)
+            + pltpu.roll(east_neg * g, 1, 0)
+            + pltpu.roll(north_pos * g, 127, 1)
+            + pltpu.roll(north_neg * g, 1, 1)
+        )
+    by_lat = product(lat_table, split(g), True)
+    adjoint = product(split(by_lat), interp, False)
+    adj_out[...] = adjoint.reshape(tiles, 8, cols)
+    adj_copies = spread_out(6, "tile", lambda dest: adj_out.at[dest], adj_in)
+    arrive(adj_copies)
+    for r in range(rows):
+        for level in range(group_levels):
+            own_adj[r, level : level + 1, :] = adj_in[level, r : r + 1, :]
+    own_copies = spread_out(1, "mem", lambda dest: own_adj, adj_all)
+    arrive(own_copies)
+
+    member_rows = []
+    for r in range(rows):
+        field = jnp.concatenate([adj_all[i, r] for i in range(mems)], axis=0)
+        member_rows.append((spread * field) * prt[r])
+    state = member_rows[rows - 1]
+    summed = [state]
+    for r in reversed(range(rows - 1)):
+        state = member_rows[r] + rate[r + 1] * state
+        summed.insert(0, state)
+    store_pieces(send_c, rate[0] * state)
+    up_copies = spread_out(7, "tile", lambda dest: send_c.at[dest], got_c)
+    smooth_rows = [smooth(shrink[r] * summed[r], True) for r in range(rows)]
+    arrive(up_copies)
+    state = jnp.zeros((members, 8, 128), f32)
+    for s in reversed(range(tiles)):
+        send_d[s] = state
+        state = gains[s] * state + got_c[s]
+    last_copies = spread_out(8, "tile", lambda dest: send_d.at[dest], got_d)
+    arrive(last_copies)
+    carried = smooth(load_pieces(got_d), True)
+    gain = None
+    for r in reversed(range(rows)):
+        gain = jnp.ones_like(rate[r]) if r == rows - 1 else gain * rate[r + 1]
+        out[r] = ctl[r] + smooth_rows[r] + (shrink[r] * gain) * carried
+    for copy in started:
+        copy.wait_send()
+
+
+def fused(
+    perturbations, control, filter_rate, lat_weight, lon_weight, wind_east, wind_north, obs_weight
+):
+    members, levels, rows, cols = control.shape
+    tiles, mems = lax.axis_size("tile"), lax.axis_size("mem")
+    t, m = lax.axis_index("tile"), lax.axis_index("mem")
+    f32 = jnp.float32
+    rows_fine, band = wind_east.shape
+    ctl = jnp.transpose(control, (2, 0, 1, 3))
+    prt = jnp.transpose(perturbations, (2, 0, 1, 3)).astype(f32)
+    lat_lane = jnp.arange(128)[None, :] - t * lat_weight.shape[0]
+    lat_slot = jnp.arange(lat_weight.shape[0])[:, None]
+    lat_row = jnp.sum(
+        jnp.where(lat_lane == lat_slot, lat_weight.astype(f32)[:, None] / 256.0, 0.0), axis=0
+    )
+    gain_row = jnp.pad(jnp.prod(filter_rate, axis=0), (0, 128 - levels))
+    small = jnp.concatenate([lat_row[None], gain_row[None], jnp.zeros((6, 128), f32)], axis=0)
+    winds = jnp.concatenate(
+        [
+            jnp.pad(jnp.transpose(w).astype(f32) / 1024.0, ((0, 0), (0, 64 - rows_fine)))
+            for w in (wind_east, wind_north)
+        ],
+        axis=1,
+    )
+    group = levels // mems
+    obs = lax.dynamic_slice_in_dim(obs_weight, m * group, group, 0)
+    obs = jnp.pad(jnp.swapaxes(obs, 1, 2), ((0, 0), (0, 0), (0, 128 - rows_fine)))
+    lon = lon_weight.astype(f32)[:, None] / 256.0
+    across = np.arange(cols)
+    distance = across[None, :] - across[:, None]
+    full = np.where(
+        distance >= 0, np.sqrt(1.0 - LON_RATE**2) * LON_RATE ** np.maximum(distance, 0.0), 0.0
+    ).astype(np.float32)
+    table_high = full.astype(ml_dtypes.bfloat16)
+    table_low = (full - table_high.astype(np.float32)).astype(ml_dtypes.bfloat16)
+    spread = float(1.0 / np.sqrt(np.float32(members * mems - 1)))
+    piece = (tiles, members, 8, 128)
+    vmem = pl.BlockSpec(memory_space=pltpu.VMEM)
+    result = pl.pallas_call(
+        functools.partial(hessian_kernel, tiles, mems, rows_fine, spread),
+        out_shape=jax.ShapeDtypeStruct(ctl.shape, f32),
+        in_specs=[vmem] * 9,
+        out_specs=vmem,
+        scratch_shapes=[
+            pltpu.VMEM((tiles, 8, 128), f32),
+            pltpu.VMEM((tiles, band, 128), f32),
+            pltpu.VMEM((tiles, band, 128), f32),
+            *[pltpu.VMEM(piece, f32)] * 4,
+            *[pltpu.VMEM((mems, rows, group, cols), f32)] * 2,
+            *[pltpu.VMEM((tiles, 8, cols), f32)] * 4,
+            pltpu.VMEM((rows, group, cols), f32),
+            pltpu.VMEM((mems, rows, group, cols), f32),
+            *[pltpu.VMEM(piece, f32)] * 4,
+            pltpu.SemaphoreType.DMA((9, tiles)),
+            pltpu.SemaphoreType.DMA((9, tiles)),
+            pltpu.SemaphoreType.DMA((2, mems)),
+            pltpu.SemaphoreType.DMA((2, mems)),
+        ],
+        compiler_params=pltpu.CompilerParams(
+            collective_id=0, has_side_effects=True, vmem_limit_bytes=40 * 2**20
+        ),
+    )(ctl, prt, filter_rate.T, small, winds, obs, lon, table_high, table_low)
+    return jnp.transpose(result, (1, 2, 0, 3))
+
+
+def plan(
+    perturbations, control, filter_rate, lat_weight, lon_weight, wind_east, wind_north, obs_weight
+):
+    levels, rows, cols = control.shape[1:]
+    tiles, mems = lax.axis_size("tile"), lax.axis_size("mem")
+    fits = (
+        levels == tiles * mems
+        and tiles == 8
+        and levels // 8 * -(-cols // 128) == tiles
+        and rows <= 8
+        and wind_east.shape[0] <= 64
+        and wind_east.shape[1] % 8 == 0
+        and levels <= 128
+    )
+    return (fused if fits else local)(
+        perturbations, control, filter_rate, lat_weight, lon_weight, wind_east, wind_north,
+        obs_weight,
+    )
+
 
 def solution(mesh):
     placed = (
@@ -209,5 +544,5 @@
         P(None, None, "tile"),
     )
     return jax.shard_map(
-        local, mesh=mesh, in_specs=placed, out_specs=P("mem", None, "tile", None), check_vma=False
-    )
+        plan, mesh=mesh, in_specs=placed, out_specs=P("mem", None, "tile", None), check_vma=False
+    )

time: 211 us -> 56.4 us (0.27)
  blocking collectives: 84.1 us -> 0 us
  waiting for transfers between devices: 53.2 us -> 0 us
  Pallas kernels: 0 us -> 50.5 us
  starting transfers between devices: 30.3 us -> 0 us
  between operations: 15.2 us -> 0.13 us
  other arithmetic: 11.3 us -> 0.25 us
  matrix products: 6.19 us -> 0 us
  local copies, waits for them, and re-layouts: 9.56 us -> 5.19 us
    pallas_call x0 -> x1, Pallas kernels: none -> 50.5 us  [fused(): pl.pallas_call(functools.partial(hessian_kernel, tiles, mems, rows_fine,...]
    unnamed x3 -> x0, blocking collectives: 39.4 us -> none
    all_gather x2 -> x0, blocking collectives: 35.9 us -> none  [carried_in(): gathered = jax.tree.map(lambda a: lax.all_gather(a, axis), part)]
    psum x1 -> x0, waiting for transfers between devices: 30 us -> none  [local(): increment = lax.psum(partial_sum, 'mem')]
    ppermute x16 -> x0, starting transfers between devices: 25 us -> none  [the longest x7 21.1 us: with_halo(): after = lax.ppermute(leading, axis, down)]
    ppermute x16 -> x0, waiting for transfers between devices: 16.8 us -> none  [the longest x7 11.7 us: with_halo(): before = lax.ppermute(last, axis, up)]
    all_to_all x1 -> x0, blocking collectives: 8.84 us -> none  [local(): lax.all_to_all(extended_adjoint, 'tile', split_axis=1, concat_axis=1, til...]
    all_to_all x1 -> x0, waiting for transfers between devices: 6.44 us -> none  [local(): lax.all_to_all(windows, 'tile', split_axis=1, concat_axis=1, tiled=True)]
  transfers between devices with their start and end apart: 18 -> 0, of which waited for: 15 -> 0; matrix products, arithmetic and copies ran while one was open for 2% -> 0% of each run, Pallas kernels for 0% -> 0%
where the time goes in v1:
time: 56.4 us; the launch traced here: 56.1 us
  Pallas kernels  50.5 us (90%)
  local copies, waits for them, and re-layouts  5.19 us (9%)
    pallas_call x1, Pallas kernels, fused(): pl.pallas_call(functools.partial(hessian_kernel, tiles, mems, rows_fine,...  50.5 us
    unnamed x25, local copies, waits for them, and re-layouts  4.22 us

profile of v1, /device:TPU:0, one launch (start us, length us, event | category | flops | bytes accessed | tf_op | source)
XLA Modules:
  0.0 56.1 jit_solution(7786884234671323085)
XLA Ops:
  0.0 0.0 copy-start
  0.0 0.0 copy-start.9
  0.0 0.0 copy-start.7
  0.0 0.0 copy-start.8
  0.0 0.7 %copy-done.9 = s32[6]{0:T(128)S(1)} copy-done((s32[6]{0:T(128)S(1)}, s32[6]{0:T(128)}, u32[]{:S(2)}) %copy-start.9) | copy-done | bytes 48
  0.7 0.0 copy-start.5
  0.7 0.1 select_reduce_fusion
  0.8 0.0 copy-done.7
  0.9 0.0 copy-done.8
  0.9 0.1 copy.20
  1.0 0.5 copy-done.5
  1.5 0.0 copy-start.6
  1.5 0.1 copy.21
  1.5 0.7 %copy-done.6 = s32[48,48]{1,0:T(8,128)S(1)} copy-done((s32[48,48]{1,0:T(8,128)S(1)}, s32[48,48]{1,0:T(8,128)}, u32[]{:S(2)}) %copy-start.6) | copy-done | bytes 9240
  2.2 0.1 copy.22
  2.3 0.1 select_maximum_fusion.winds
  2.4 0.1 div.29.lon
  2.5 0.0 copy-done
  2.5 0.1 copy.26
  2.6 0.0 copy-start.4
  2.7 0.0 copy-start.3
  2.7 0.9 %copy-done.4 = bf16[5,32,3,192]{3,1,2,0:T(8,128)(2,1)S(1)} copy-done((bf16[5,32,3,192]{3,1,2,0:T(8,128)(2,1)S(1)}, bf16[5,32,3,192]{3,1,2,0:T(8,128)(2,1)}, u32[]{:S(2)}) %copy-start.4) | copy-done | bytes 184344
  3.6 0.2 copy-done.3
  3.8 0.0 copy-start.1
  3.8 0.0 copy-start.2
  3.9 0.9 %copy-done.1 = bf16[192,192]{1,0:T(8,128)(2,1)S(1)} copy-done((bf16[192,192]{1,0:T(8,128)(2,1)S(1)}, bf16[192,192]{1,0:T(8,128)(2,1)}, u32[]{:S(2)}) %copy-start.1) | copy-done | bytes 73752
  4.7 0.0 copy-done.2
  4.8 50.5 %shard_map.100 = f32[3,5,32,192]{3,2,1,0:T(8,128)S(1)} custom-call(f32[3,5,32,192]{3,2,1,0:T(8,128)S(1)} %bitcast.16, f32[3,5,32,192]{3,2,1,0:T(8,128)S(1)} %convert_bitcast_fusion.prt, f32[32,3]{1,0:T(8,128)S(1)} %bitcast.17, f32[8,128]{1,0:T(8,128)S(1)} %pad_maximum_fusion.small, f32[48,128]{1,0:T(8,128)S(1)} %select_maximum_fusion.winds, ...), custom_call_target="tpu_custom_call" | custom-call | tf_op jit(solution)/shard_map/pallas_call | solution.py:488
  55.3 0.8 %copy.25 = f32[5,32,3,192]{3,1,2,0:T(8,128)} copy(f32[5,32,3,192]{3,1,0,2:T(8,128)S(1)} %bitcast.15) | data formatting | bytes 737280 | tf_op jit(solution)/shard_map/transpose | solution.py:512
  (12 shorter events, 0.2 us)
Async XLA Ops:
  0.0 2.5 %copy-start = (f32[32,48,48]{2,1,0:T(8,128)S(1)}, f32[32,48,48]{2,1,0:T(8,128)}, u32[]{:S(2)}) copy-start(f32[32,48,48]{2,1,0:T(8,128)} %param.17) | copy-start | bytes 884740
  0.0 0.7 %copy-start.9 = (s32[6]{0:T(128)S(1)}, s32[6]{0:T(128)}, u32[]{:S(2)}) copy-start(s32[6]{0:T(128)} %param.13) | copy-start | bytes 76
  0.0 0.8 %copy-start.7 = (f32[3,32]{1,0:T(4,128)S(1)}, f32[3,32]{1,0:T(4,128)}, u32[]{:S(2)}) copy-start(f32[3,32]{1,0:T(4,128)} %param.12) | copy-start | bytes 1156
  0.0 0.9 %copy-start.8 = (s32[384]{0:T(512)S(1)}, s32[384]{0:T(512)}, u32[]{:S(2)}) copy-start(s32[384]{0:T(512)} %param.14) | copy-start | bytes 4612
  0.7 0.7 %copy-start.5 = (s32[48,48]{1,0:T(8,128)S(1)}, s32[48,48]{1,0:T(8,128)}, u32[]{:S(2)}) copy-start(s32[48,48]{1,0:T(8,128)} %param.15) | copy-start | bytes 27652
  1.5 0.7 %copy-start.6 = (s32[48,48]{1,0:T(8,128)S(1)}, s32[48,48]{1,0:T(8,128)}, u32[]{:S(2)}) copy-start(s32[48,48]{1,0:T(8,128)} %param.16) | copy-start | bytes 27652
  2.6 1.0 %copy-start.4 = (bf16[5,32,3,192]{3,1,2,0:T(8,128)(2,1)S(1)}, bf16[5,32,3,192]{3,1,2,0:T(8,128)(2,1)}, u32[]{:S(2)}) copy-start(bf16[5,32,3,192]{3,1,2,0:T(8,128)(2,1)} %param.10) | copy-start | bytes 552964
  2.7 1.2 %copy-start.3 = (f32[5,32,3,192]{3,1,2,0:T(8,128)S(1)}, f32[5,32,3,192]{3,1,2,0:T(8,128)}, u32[]{:S(2)}) copy-start(f32[5,32,3,192]{3,1,2,0:T(8,128)} %param.11) | copy-start | bytes 1105924
  3.8 0.9 %copy-start.1 = (bf16[192,192]{1,0:T(8,128)(2,1)S(1)}, bf16[192,192]{1,0:T(8,128)(2,1)}, u32[]{:S(2)}) copy-start(bf16[192,192]{1,0:T(8,128)(2,1)} %constant.36.clone.table_low) | copy-start | bytes 221188
  3.8 0.9 %copy-start.2 = (bf16[192,192]{1,0:T(8,128)(2,1)S(1)}, bf16[192,192]{1,0:T(8,128)(2,1)}, u32[]{:S(2)}) copy-start(bf16[192,192]{1,0:T(8,128)(2,1)} %constant.35.clone.table_high) | copy-start | bytes 221188

commit v2 on v1

--- a/solution.py
+++ b/solution.py
@@ -1,8 +1,8 @@
 import functools
+import math
 
 import jax
 import jax.numpy as jnp
-import ml_dtypes
 import numpy as np
 from jax import lax
 from jax.experimental import pallas as pl
@@ -223,19 +223,60 @@
     return total
 
 
+def expand(ref, count):
+    return jnp.concatenate(
+        [jnp.broadcast_to(ref[q : q + 1, :], (8, 128))[None] for q in range(count)], axis=0
+    )
+
+
+def wide(x):
+    pad = jnp.zeros(x.shape[:-1] + (128 - x.shape[-1],), x.dtype)
+    return jnp.concatenate([x, pad], axis=x.ndim - 1)
+
+
+def placed_at(x, source, target, width):
+    moved = pltpu.roll(x, (target - source) % 128, 1)
+    lane = lax.broadcasted_iota(jnp.int32, x.shape, 1)
+    return jnp.where((lane >= target) & (lane < target + width), moved, 0.0)
+
+
+def column(row):
+    count = row.shape[1]
+    sub = lax.broadcasted_iota(jnp.int32, (count, count), 0)
+    lane = lax.broadcasted_iota(jnp.int32, (count, count), 1)
+    return jnp.sum(jnp.where(sub == lane, row, 0.0), axis=1, keepdims=True)
+
+
 def hessian_kernel(
-    tiles, mems, rows_fine, spread,
-    ctl, prt, rates, small, winds, obs, lon, table_high, table_low,
+    tiles, mems, spread,
+    ctl_hbm, prt_hbm, rates_hbm, lat_hbm, lon_hbm, east_hbm, north_hbm, obs_hbm,
     out,
-    smalls, winds_all, obs_all, send_a, got_a, send_b, got_b, parts, parts_got,
-    levels_out, levels_in, adj_out, adj_in, own_adj, adj_all, send_c, got_c, send_d, got_d,
-    tile_send, tile_recv, mem_send, mem_recv,
+    ctl, prt, rates, lat_in, lon_in, east_in, north_in, obs_in,
+    small, smalls, halo_out, halo_in, wind_rows, weights, send_a, got_a, send_b, got_b,
+    parts, parts_got, rows_out, rows_in, adj_out, adj_in, own_adj, adj_all,
+    send_c, got_c, send_d, got_d, interp,
+    local_sem, halo_send, halo_recv, tile_send, tile_recv, mem_send, mem_recv,
 ):
-    rows, members, levels, cols = ctl.shape
+    members, rows, levels, cols = ctl.shape
     t = lax.axis_index("tile")
     m = lax.axis_index("mem")
     f32 = jnp.float32
     started = []
+    group_levels = levels // mems
+    rows_fine, band = east_in.shape
+    halo = 2 * STEPS
+    width = band + 2 * halo
+
+    loads = []
+    sources = (
+        (rates_hbm, rates), (ctl_hbm, ctl), (lat_hbm, lat_in), (east_hbm, east_in),
+        (north_hbm, north_in), (obs_hbm.at[pl.ds(m * group_levels, group_levels)], obs_in),
+        (lon_hbm, lon_in), (prt_hbm, prt),
+    )
+    for i, (source, target) in enumerate(sources):
+        load = pltpu.make_async_copy(source, target, local_sem.at[i])
+        load.start()
+        loads.append(load)
 
     barrier = pltpu.get_barrier_semaphore()
     for d in range(1, tiles):
@@ -271,46 +312,83 @@
         for copy in copies:
             copy.wait_recv()
 
-    rate = [rates[:, r : r + 1] for r in range(rows)]
-    shrink = [jnp.sqrt(1.0 - a * a) for a in rate]
-
     def store_pieces(target, value):
         for lane_part in range(-(-cols // 128)):
             low = 128 * lane_part
-            width = min(128, cols - low)
+            span = min(128, cols - low)
             for group in range(levels // 8):
                 piece = lane_part * (levels // 8) + group
-                block = value[:, 8 * group : 8 * group + 8, low : low + width]
-                if width < 128:
-                    block = jnp.concatenate(
-                        [block, jnp.zeros((members, 8, 128 - width), f32)], axis=2
-                    )
-                target[piece] = block
+                block = value[:, 8 * group : 8 * group + 8, low : low + span]
+                target[piece] = wide(block) if span < 128 else block
 
     def load_pieces(source):
         groups = levels // 8
         lanes = []
         for lane_part in range(-(-cols // 128)):
-            width = min(128, cols - 128 * lane_part)
+            span = min(128, cols - 128 * lane_part)
             blocks = [source[lane_part * groups + g] for g in range(groups)]
-            lanes.append(jnp.concatenate(blocks, axis=1)[:, :, :width])
+            lanes.append(jnp.concatenate(blocks, axis=1)[:, :, :span])
         return jnp.concatenate(lanes, axis=2)
 
+    loads[0].wait()
+    rate = [column(rates[r : r + 1, :]) for r in range(rows)]
+    shrink = [jnp.sqrt(1.0 - a * a) for a in rate]
+    gain_row = rates[0:1, :]
+    for r in range(1, rows):
+        gain_row = gain_row * rates[r : r + 1, :]
+    loads[1].wait()
     local_rows = []
     state = None
     for r in range(rows):
-        term = shrink[r] * ctl[r]
+        term = shrink[r] * ctl[:, r]
         state = term if r == 0 else rate[r] * state + term
         local_rows.append(state)
     store_pieces(send_a, state)
+    loads[2].wait()
+    small[...] = jnp.zeros_like(small)
+    small[0 : 2 * rows, :] = jnp.broadcast_to(
+        column(lat_in[...].astype(f32)) / 256.0, (2 * rows, 128)
+    )
+    small[2 * rows : 2 * rows + 1, :] = wide(gain_row)
 
     pl.semaphore_wait(barrier, tiles - 1 + mems - 1)
+    carry_copies = spread_out(1, "tile", lambda dest: send_a.at[dest], got_a)
     small_copies = spread_out(0, "tile", lambda dest: small, smalls)
-    carry_copies = spread_out(1, "tile", lambda dest: send_a.at[dest], got_a)
-    wind_copies = spread_out(2, "tile", lambda dest: winds, winds_all)
-    obs_copies = spread_out(3, "tile", lambda dest: obs.at[dest], obs_all)
-
-    table = (table_high[...], table_low[...])
+
+    for load in loads[3:]:
+        load.wait()
+    east_own = wide(east_in[...].astype(f32) / 1024.0)
+    north_own = wide(north_in[...].astype(f32) / 1024.0)
+    edges = jnp.zeros((rows_fine, 128), f32)
+    for i, wind in enumerate((east_own, north_own)):
+        edges = edges + placed_at(wind, 0, 2 * halo * i, halo)
+        edges = edges + placed_at(wind, band - halo, 2 * halo * i + halo, halo)
+    base = 4 * halo
+    for level in range(group_levels):
+        slab = wide(obs_in[level])
+        at = base + 2 * STEPS * level
+        edges = edges + placed_at(slab, 0, at, STEPS)
+        edges = edges + placed_at(slab, band - STEPS, at + STEPS, STEPS)
+    halo_out[...] = edges
+    halo_copies = []
+    for side, d in enumerate((1, tiles - 1)):
+        copy = pltpu.make_async_remote_copy(
+            src_ref=halo_out,
+            dst_ref=halo_in.at[side],
+            send_sem=halo_send.at[side],
+            recv_sem=halo_recv.at[side],
+            device_id={"tile": lax.rem(t + d, tiles)},
+            device_id_type=MESH,
+        )
+        copy.start()
+        halo_copies.append(copy)
+    started.extend(halo_copies)
+
+    sub = lax.broadcasted_iota(jnp.int32, (cols, cols), 0)
+    lane = lax.broadcasted_iota(jnp.int32, (cols, cols), 1)
+    apart = (lane - sub).astype(f32)
+    powers = jnp.exp(jnp.maximum(apart, 0.0) * math.log(LON_RATE))
+    table = split(jnp.where(lane >= sub, math.sqrt(1.0 - LON_RATE**2) * powers, 0.0))
 
     def smooth(x, turned):
         flat = x.reshape(members * levels, cols)
@@ -325,124 +403,145 @@
     gain_mask = lane == sub + 8 * group
     gains = []
     for s in range(tiles):
-        row = smalls[s, 1:2, :]
+        row = smalls[s, 2 * rows : 2 * rows + 1, :]
         gains.append(jnp.sum(jnp.where(gain_mask, row, 0.0), axis=1, keepdims=True))
     arrive(carry_copies)
     state = jnp.zeros((members, 8, 128), f32)
     for s in range(tiles):
         send_b[s] = state
         state = gains[s] * state + got_a[s]
-    back_copies = spread_out(4, "tile", lambda dest: send_b.at[dest], got_b)
-
-    levels_out[...] = jnp.zeros_like(levels_out)
-    interp_row = lax.broadcasted_iota(jnp.int32, (lon.shape[0], cols), 0) // 2
-    interp_col = lax.broadcasted_iota(jnp.int32, (lon.shape[0], cols), 1)
-    west = lon[...]
-    interp = jnp.where(interp_col == interp_row, west, 0.0) + jnp.where(
-        interp_col == lax.rem(interp_row + 1, cols), 1.0 - west, 0.0
-    )
-    interp = (interp.astype(jnp.bfloat16),)
-    lat = smalls[0, 0:1, :]
-    for s in range(1, tiles):
-        lat = lat + smalls[s, 0:1, :]
-    slot = lax.broadcasted_iota(jnp.int32, (8 * tiles, 128), 0)
-    fine_row = lax.broadcasted_iota(jnp.int32, (8 * tiles, 128), 1) // 2
-    coarse = jnp.where(slot % 8 < rows, slot // 8 * rows + slot % 8, -2)
-    inside = fine_row < rows * tiles
-    lat_table = jnp.where((fine_row == coarse) & inside, lat, 0.0) + jnp.where(
-        (fine_row + 1 == coarse) & inside, 1.0 - lat, 0.0
-    )
-    lat_table = (lat_table.astype(jnp.bfloat16),)
+    back_copies = spread_out(2, "tile", lambda dest: send_b.at[dest], got_b)
+
+    count = lon_in.shape[1]
+    lon_row = jnp.broadcast_to(lon_in[...].astype(f32) / 256.0, (8, count))
+    slot = lax.broadcasted_iota(jnp.int32, (cols, 128), 0)
+    lane = lax.broadcasted_iota(jnp.int32, (cols, 128), 1)
+    for i in range(tiles):
+        west = pltpu.roll(lon_row, (halo - band * i) % count, 1)[0:1, :128]
+        lower = lax.rem(lane + (band * i - halo + count), count) // 2
+        upper = lax.rem(lower + 1, cols)
+        weight = jnp.where(slot == lower, west, 0.0) + jnp.where(slot == upper, 1.0 - west, 0.0)
+        weight = jnp.where(lane < width, weight, 0.0)
+        interp[:, 128 * i : 128 * (i + 1)] = weight.astype(jnp.bfloat16)
+    arrive(halo_copies)
+    from_west, from_east = halo_in[0], halo_in[1]
+    for i, wind in enumerate((east_own, north_own)):
+        wind_rows[i] = (
+            placed_at(wind, 0, halo, band)
+            + placed_at(from_west, (2 * i + 1) * halo, 0, halo)
+            + placed_at(from_east, 2 * i * halo, halo + band, halo)
+        )
+    slabs = []
+    for level in range(group_levels):
+        at = base + 2 * STEPS * level
+        slab = placed_at(wide(obs_in[level]), 0, halo, band)
+        slab = slab + placed_at(from_west, at + STEPS, halo - STEPS, STEPS)
+        slab = slab + placed_at(from_east, at, halo + band, STEPS)
+        slabs.append(slab[None])
+    weights[...] = jnp.swapaxes(jnp.concatenate(slabs, axis=0), 0, 1)
 
     arrive(back_copies)
     carried = smooth(load_pieces(got_b), False)
     gain = None
-    group_levels = levels // mems
     for r in range(rows):
         gain = rate[r] if r == 0 else gain * rate[r]
         localized = gain * carried + smooth_rows[r]
-        partial = spread * jnp.sum(prt[r] * localized, axis=0)
+        partial = spread * jnp.sum(prt[:, r].astype(f32) * localized, axis=0)
         for i in range(mems):
-            parts[i, r] = partial[i * group_levels : (i + 1) * group_levels]
+            parts[i, 8 * r : 8 * r + 8] = partial[i * group_levels : (i + 1) * group_levels]
     part_copies = spread_out(0, "mem", lambda dest: parts.at[dest], parts_got)
-
-    arrive(wind_copies)
-    arrive(obs_copies)
-    count = lon.shape[0]
-    both = winds_all[...].reshape(count, 128)
-    keep_lane = lax.broadcasted_iota(jnp.int32, (count, 128), 1) < rows_fine
-    east = jnp.where(keep_lane, both, 0.0)
-    north = jnp.where(keep_lane, pltpu.roll(both, 64, 1), 0.0)
+    east = expand(wind_rows.at[0], rows_fine)
+    north = expand(wind_rows.at[1], rows_fine)
     east_pos = jnp.maximum(east, 0.0)
     east_neg = jnp.maximum(-east, 0.0)
     north_pos = jnp.maximum(north, 0.0)
     north_neg = jnp.maximum(-north, 0.0)
     keep = 1.0 - east_pos - east_neg - north_pos - north_neg
+    lat = jnp.concatenate([expand(smalls.at[s], 2 * rows) for s in range(tiles)], axis=0)
     arrive(part_copies)
-    for r in range(rows):
-        total = parts_got[0, r]
-        for i in range(1, mems):
-            total = total + parts_got[i, r]
-        for level in range(group_levels):
-            levels_out[level, r : r + 1, :] = total[level : level + 1, :]
-    level_copies = spread_out(5, "tile", lambda dest: levels_out.at[dest], levels_in)
-    arrive(level_copies)
-
-    increment = levels_in[...].reshape(8 * tiles, cols)
-    by_lon = product(interp, split(increment), True)
-    g = product(split(by_lon), lat_table, False)
+    total = parts_got[0]
+    for i in range(1, mems):
+        total = total + parts_got[i]
+    every = product(split(total), (interp[...],), False)
+    for i in range(tiles):
+        rows_out[i] = every[:, 128 * i : 128 * (i + 1)]
+    row_copies = spread_out(3, "tile", lambda dest: rows_out.at[dest], rows_in)
+    arrive(row_copies)
+
+    coarse = tiles * rows
+    edge = jnp.zeros((1, 8, 128), f32)
+
+    def southward(x):
+        return jnp.concatenate([edge, x[:-1]], axis=0)
+
+    def northward(x):
+        return jnp.concatenate([x[1:], edge], axis=0)
+
+    def doubled(x):
+        return jnp.broadcast_to(x[:, None], (coarse, 2, 8, 128)).reshape(rows_fine, 8, 128)
+
+    def paired(x):
+        pairs = x.reshape(coarse, 2, 8, 128)
+        return pairs[:, 0] + pairs[:, 1]
+
+    def turn(x, distance):
+        flat = x.reshape(rows_fine * 8, 128)
+        return pltpu.roll(flat, distance, 1).reshape(rows_fine, 8, 128)
+
+    increment = rows_in[...].reshape(coarse, 8, 128)
+    g = lat * doubled(increment) + (1.0 - lat) * doubled(northward(increment))
     for _ in range(STEPS):
         g = (
             keep * g
-            + east_pos * pltpu.roll(g, 1, 0)
-            + east_neg * pltpu.roll(g, count - 1, 0)
-            + north_pos * pltpu.roll(g, 1, 1)
-            + north_neg * pltpu.roll(g, 127, 1)
+            + east_pos * turn(g, 1)
+            + east_neg * turn(g, 127)
+            + north_pos * southward(g)
+            + north_neg * northward(g)
         )
-    g = obs_all[...].reshape(count, 128) * g
+    g = weights[...] * g
     for _ in range(STEPS):
         g = (
             keep * g
-            + pltpu.roll(east_pos * g, count - 1, 0)
-            + pltpu.roll(east_neg * g, 1, 0)
-            + pltpu.roll(north_pos * g, 127, 1)
-            + pltpu.roll(north_neg * g, 1, 1)
+            + turn(east_pos * g, 127)
+            + turn(east_neg * g, 1)
+            + northward(north_pos * g)
+            + southward(north_neg * g)
         )
-    by_lat = product(lat_table, split(g), True)
-    adjoint = product(split(by_lat), interp, False)
-    adj_out[...] = adjoint.reshape(tiles, 8, cols)
-    adj_copies = spread_out(6, "tile", lambda dest: adj_out.at[dest], adj_in)
+    lane = lax.broadcasted_iota(jnp.int32, g.shape, 2)
+    g = jnp.where((lane >= halo) & (lane < halo + band), g, 0.0)
+    adjoint = paired(lat * g) + southward(paired((1.0 - lat) * g))
+    adj_out[...] = adjoint.reshape(tiles, rows * 8, 128)
+    adj_copies = spread_out(4, "tile", lambda dest: adj_out.at[dest], adj_in)
     arrive(adj_copies)
-    for r in range(rows):
-        for level in range(group_levels):
-            own_adj[r, level : level + 1, :] = adj_in[level, r : r + 1, :]
+    every = jnp.concatenate([adj_in[i] for i in range(tiles)], axis=1)
+    own_adj[...] = product(split(every), (interp[...],), True)
     own_copies = spread_out(1, "mem", lambda dest: own_adj, adj_all)
     arrive(own_copies)
 
     member_rows = []
     for r in range(rows):
-        field = jnp.concatenate([adj_all[i, r] for i in range(mems)], axis=0)
-        member_rows.append((spread * field) * prt[r])
+        field = jnp.concatenate([adj_all[i, 8 * r : 8 * r + 8] for i in range(mems)], axis=0)
+        member_rows.append((spread * field) * prt[:, r].astype(f32))
     state = member_rows[rows - 1]
     summed = [state]
     for r in reversed(range(rows - 1)):
         state = member_rows[r] + rate[r + 1] * state
         summed.insert(0, state)
     store_pieces(send_c, rate[0] * state)
-    up_copies = spread_out(7, "tile", lambda dest: send_c.at[dest], got_c)
+    up_copies = spread_out(5, "tile", lambda dest: send_c.at[dest], got_c)
     smooth_rows = [smooth(shrink[r] * summed[r], True) for r in range(rows)]
     arrive(up_copies)
     state = jnp.zeros((members, 8, 128), f32)
     for s in reversed(range(tiles)):
         send_d[s] = state
         state = gains[s] * state + got_c[s]
-    last_copies = spread_out(8, "tile", lambda dest: send_d.at[dest], got_d)
+    last_copies = spread_out(6, "tile", lambda dest: send_d.at[dest], got_d)
     arrive(last_copies)
     carried = smooth(load_pieces(got_d), True)
     gain = None
     for r in reversed(range(rows)):
         gain = jnp.ones_like(rate[r]) if r == rows - 1 else gain * rate[r + 1]
-        out[r] = ctl[r] + smooth_rows[r] + (shrink[r] * gain) * carried
+        out[:, r] = ctl[:, r] + smooth_rows[r] + (shrink[r] * gain) * carried
     for copy in started:
         copy.wait_send()
 
@@ -452,64 +551,58 @@
 ):
     members, levels, rows, cols = control.shape
     tiles, mems = lax.axis_size("tile"), lax.axis_size("mem")
-    t, m = lax.axis_index("tile"), lax.axis_index("mem")
-    f32 = jnp.float32
+    f32, i32 = jnp.float32, jnp.int32
     rows_fine, band = wind_east.shape
-    ctl = jnp.transpose(control, (2, 0, 1, 3))
-    prt = jnp.transpose(perturbations, (2, 0, 1, 3)).astype(f32)
-    lat_lane = jnp.arange(128)[None, :] - t * lat_weight.shape[0]
-    lat_slot = jnp.arange(lat_weight.shape[0])[:, None]
-    lat_row = jnp.sum(
-        jnp.where(lat_lane == lat_slot, lat_weight.astype(f32)[:, None] / 256.0, 0.0), axis=0
-    )
-    gain_row = jnp.pad(jnp.prod(filter_rate, axis=0), (0, 128 - levels))
-    small = jnp.concatenate([lat_row[None], gain_row[None], jnp.zeros((6, 128), f32)], axis=0)
-    winds = jnp.concatenate(
-        [
-            jnp.pad(jnp.transpose(w).astype(f32) / 1024.0, ((0, 0), (0, 64 - rows_fine)))
-            for w in (wind_east, wind_north)
-        ],
-        axis=1,
-    )
+    ctl = jnp.transpose(control, (0, 2, 1, 3))
+    prt = jnp.transpose(perturbations, (0, 2, 1, 3))
     group = levels // mems
-    obs = lax.dynamic_slice_in_dim(obs_weight, m * group, group, 0)
-    obs = jnp.pad(jnp.swapaxes(obs, 1, 2), ((0, 0), (0, 0), (0, 128 - rows_fine)))
-    lon = lon_weight.astype(f32)[:, None] / 256.0
-    across = np.arange(cols)
-    distance = across[None, :] - across[:, None]
-    full = np.where(
-        distance >= 0, np.sqrt(1.0 - LON_RATE**2) * LON_RATE ** np.maximum(distance, 0.0), 0.0
-    ).astype(np.float32)
-    table_high = full.astype(ml_dtypes.bfloat16)
-    table_low = (full - table_high.astype(np.float32)).astype(ml_dtypes.bfloat16)
     spread = float(1.0 / np.sqrt(np.float32(members * mems - 1)))
-    piece = (tiles, members, 8, 128)
-    vmem = pl.BlockSpec(memory_space=pltpu.VMEM)
+    piece = pltpu.VMEM((tiles, members, 8, 128), f32)
+    partial = pltpu.VMEM((mems, rows * group, cols), f32)
+    window = pltpu.VMEM((tiles, rows * group, 128), f32)
     result = pl.pallas_call(
-        functools.partial(hessian_kernel, tiles, mems, rows_fine, spread),
+        functools.partial(hessian_kernel, tiles, mems, spread),
         out_shape=jax.ShapeDtypeStruct(ctl.shape, f32),
-        in_specs=[vmem] * 9,
-        out_specs=vmem,
+        in_specs=[pl.BlockSpec(memory_space=pl.ANY)] * 8,
+        out_specs=pl.BlockSpec(memory_space=pltpu.VMEM),
         scratch_shapes=[
+            pltpu.VMEM(ctl.shape, f32),
+            pltpu.VMEM(prt.shape, prt.dtype),
+            pltpu.VMEM(filter_rate.shape, f32),
+            pltpu.VMEM((1, lat_weight.shape[0]), i32),
+            pltpu.VMEM((1, lon_weight.shape[0]), i32),
+            pltpu.VMEM((rows_fine, band), i32),
+            pltpu.VMEM((rows_fine, band), i32),
+            pltpu.VMEM((group, rows_fine, band), f32),
+            pltpu.VMEM((8, 128), f32),
             pltpu.VMEM((tiles, 8, 128), f32),
-            pltpu.VMEM((tiles, band, 128), f32),
-            pltpu.VMEM((tiles, band, 128), f32),
-            *[pltpu.VMEM(piece, f32)] * 4,
-            *[pltpu.VMEM((mems, rows, group, cols), f32)] * 2,
-            *[pltpu.VMEM((tiles, 8, cols), f32)] * 4,
-            pltpu.VMEM((rows, group, cols), f32),
-            pltpu.VMEM((mems, rows, group, cols), f32),
-            *[pltpu.VMEM(piece, f32)] * 4,
-            pltpu.SemaphoreType.DMA((9, tiles)),
-            pltpu.SemaphoreType.DMA((9, tiles)),
+            pltpu.VMEM((rows_fine, 128), f32),
+            pltpu.VMEM((2, rows_fine, 128), f32),
+            pltpu.VMEM((2, rows_fine, 128), f32),
+            pltpu.VMEM((rows_fine, group, 128), f32),
+            *[piece] * 4,
+            *[partial] * 2,
+            *[window] * 4,
+            pltpu.VMEM((rows * group, cols), f32),
+            partial,
+            *[piece] * 4,
+            pltpu.VMEM((cols, tiles * 128), jnp.bfloat16),
+            pltpu.SemaphoreType.DMA((8,)),
+            pltpu.SemaphoreType.DMA((2,)),
+            pltpu.SemaphoreType.DMA((2,)),
+            pltpu.SemaphoreType.DMA((7, tiles)),
+            pltpu.SemaphoreType.DMA((7, tiles)),
             pltpu.SemaphoreType.DMA((2, mems)),
             pltpu.SemaphoreType.DMA((2, mems)),
         ],
         compiler_params=pltpu.CompilerParams(
             collective_id=0, has_side_effects=True, vmem_limit_bytes=40 * 2**20
         ),
-    )(ctl, prt, filter_rate.T, small, winds, obs, lon, table_high, table_low)
-    return jnp.transpose(result, (1, 2, 0, 3))
+    )(
+        ctl, prt, filter_rate, lat_weight[None], lon_weight[None], wind_east, wind_north,
+        obs_weight,
+    )
+    return jnp.transpose(result, (0, 2, 1, 3))
 
 
 def plan(
@@ -517,13 +610,15 @@
 ):
     levels, rows, cols = control.shape[1:]
     tiles, mems = lax.axis_size("tile"), lax.axis_size("mem")
+    rows_fine, band = wind_east.shape
     fits = (
-        levels == tiles * mems
-        and tiles == 8
+        levels == 8 * mems
         and levels // 8 * -(-cols // 128) == tiles
-        and rows <= 8
-        and wind_east.shape[0] <= 64
-        and wind_east.shape[1] % 8 == 0
+        and tiles > 2
+        and 2 * rows + 1 <= 8
+        and rows_fine == 2 * rows * tiles
+        and rows_fine % 8 == 0
+        and 2 * STEPS <= band <= 128 - 4 * STEPS
         and levels <= 128
     )
     return (fused if fits else local)(

time: 56.4 us -> 52.3 us (0.927)
  Pallas kernels: 50.5 us -> 45.2 us
  local copies, waits for them, and re-layouts: 5.19 us -> 6.72 us
    pallas_call x1, Pallas kernels: 50.5 us -> 45.2 us  [fused(): pl.pallas_call(functools.partial(hessian_kernel, tiles, mems, spread), ou...]
    unnamed x25 -> x17, local copies, waits for them, and re-layouts: 4.22 us -> 6.72 us
    transpose x1 -> x0, local copies, waits for them, and re-layouts: 0.81 us -> none  [fused(): return jnp.transpose(result, (1, 2, 0, 3))]
where the time goes in v2:
time: 52.3 us; the launch traced here: 51.9 us
  Pallas kernels  45.2 us (86%)
  local copies, waits for them, and re-layouts  6.72 us (13%)
    pallas_call x1, Pallas kernels, fused(): pl.pallas_call(functools.partial(hessian_kernel, tiles, mems, spread), ou...  45.2 us
    unnamed x17, local copies, waits for them, and re-layouts  6.72 us

profile of v2, /device:TPU:0, one launch (start us, length us, event | category | flops | bytes accessed | tf_op | source)
XLA Modules:
  0.0 51.9 jit_solution(5244300100597438193)
XLA Ops:
  0.0 0.0 copy-start.7
  0.0 0.7 %copy-done.7 = s32[384]{0:T(512)S(1)} copy-done((s32[384]{0:T(512)S(1)}, s32[384]{0:T(512)}, u32[]{:S(2)}) %copy-start.7) | copy-done | bytes 1560
  0.7 0.0 copy-start.5
  0.7 0.0 copy-start.6
  0.7 0.7 %copy-done.5 = f32[3,32]{1,0:T(4,128)S(1)} copy-done((f32[3,32]{1,0:T(4,128)S(1)}, f32[3,32]{1,0:T(4,128)}, u32[]{:S(2)}) %copy-start.5) | copy-done | bytes 408
  1.4 0.0 copy-done.6
  1.4 0.0 copy-start
  1.4 1.1 %copy-done = f32[32,48,48]{2,1,0:T(8,128)S(1)} copy-done((f32[32,48,48]{2,1,0:T(8,128)S(1)}, f32[32,48,48]{2,1,0:T(8,128)}, u32[]{:S(2)}) %copy-start) | copy-done | bytes 294936
  2.5 0.0 copy-start.1
  2.5 1.0 %copy-done.1 = f32[5,32,3,192]{3,1,2,0:T(8,128)S(1)} copy-done((f32[5,32,3,192]{3,1,2,0:T(8,128)S(1)}, f32[5,32,3,192]{3,1,2,0:T(8,128)}, u32[]{:S(2)}) %copy-start.1) | copy-done | bytes 368664
  3.5 0.0 copy-start.2
  3.5 0.9 %copy-done.2 = bf16[5,32,3,192]{3,1,2,0:T(8,128)(2,1)S(1)} copy-done((bf16[5,32,3,192]{3,1,2,0:T(8,128)(2,1)S(1)}, bf16[5,32,3,192]{3,1,2,0:T(8,128)(2,1)}, u32[]{:S(2)}) %copy-start.2) | copy-done | bytes 184344
  4.5 0.0 copy-start.3
  4.5 0.7 %copy-done.3 = s32[48,48]{1,0:T(8,128)S(1)} copy-done((s32[48,48]{1,0:T(8,128)S(1)}, s32[48,48]{1,0:T(8,128)}, u32[]{:S(2)}) %copy-start.3) | copy-done | bytes 9240
  5.2 0.0 copy-start.4
  5.2 0.7 %copy-done.4 = s32[48,48]{1,0:T(8,128)S(1)} copy-done((s32[48,48]{1,0:T(8,128)S(1)}, s32[48,48]{1,0:T(8,128)}, u32[]{:S(2)}) %copy-start.4) | copy-done | bytes 9240
  6.0 45.2 %shard_map.82 = f32[5,3,32,192]{3,2,1,0:T(8,128)S(1)} custom-call(f32[5,3,32,192]{3,2,1,0:T(8,128)S(1)} %bitcast.5, bf16[5,3,32,192]{3,2,1,0:T(8,128)(2,1)S(1)} %bitcast.6, f32[3,32]{1,0:T(4,128)S(1)} %copy-done.5, s32[1,6]{1,0:T(1,128)S(1)} %bitcast.7, s32[1,384]{1,0:T(1,128)S(1)} %broadcast_in_dim.7.lon_hbm, s32[48,48]{1,0:T(8,128)S(1)} %copy-done.3, ...), custom_call_target="tpu_custom_call" | custom-call | tf_op jit(solution)/shard_map/pallas_call | solution.py:563
  51.2 0.8 %copy.10 = f32[5,32,3,192]{3,1,2,0:T(8,128)} copy(f32[5,32,3,192]{3,1,2,0:T(8,128)S(1)} %bitcast.4) | data formatting | bytes 737280
  (1 shorter events, 0.0 us)
Async XLA Ops:
  0.0 0.7 %copy-start.7 = (s32[384]{0:T(512)S(1)}, s32[384]{0:T(512)}, u32[]{:S(2)}) copy-start(s32[384]{0:T(512)} %param.12) | copy-start | bytes 4612
  0.7 0.7 %copy-start.5 = (f32[3,32]{1,0:T(4,128)S(1)}, f32[3,32]{1,0:T(4,128)}, u32[]{:S(2)}) copy-start(f32[3,32]{1,0:T(4,128)} %rates_hbm.1) | copy-start | bytes 1156
  0.7 0.7 %copy-start.6 = (s32[6]{0:T(128)S(1)}, s32[6]{0:T(128)}, u32[]{:S(2)}) copy-start(s32[6]{0:T(128)} %param.11) | copy-start | bytes 76
  1.4 1.1 %copy-start = (f32[32,48,48]{2,1,0:T(8,128)S(1)}, f32[32,48,48]{2,1,0:T(8,128)}, u32[]{:S(2)}) copy-start(f32[32,48,48]{2,1,0:T(8,128)} %obs_hbm.1) | copy-start | bytes 884740
  2.5 1.0 %copy-start.1 = (f32[5,32,3,192]{3,1,2,0:T(8,128)S(1)}, f32[5,32,3,192]{3,1,2,0:T(8,128)}, u32[]{:S(2)}) copy-start(f32[5,32,3,192]{3,1,2,0:T(8,128)} %param.9) | copy-start | bytes 1105924
  3.5 0.9 %copy-start.2 = (bf16[5,32,3,192]{3,1,2,0:T(8,128)(2,1)S(1)}, bf16[5,32,3,192]{3,1,2,0:T(8,128)(2,1)}, u32[]{:S(2)}) copy-start(bf16[5,32,3,192]{3,1,2,0:T(8,128)(2,1)} %param.8) | copy-start | bytes 552964
  4.5 0.7 %copy-start.3 = (s32[48,48]{1,0:T(8,128)S(1)}, s32[48,48]{1,0:T(8,128)}, u32[]{:S(2)}) copy-start(s32[48,48]{1,0:T(8,128)} %east_hbm.1) | copy-start | bytes 27652
  5.2 0.7 %copy-start.4 = (s32[48,48]{1,0:T(8,128)S(1)}, s32[48,48]{1,0:T(8,128)}, u32[]{:S(2)}) copy-start(s32[48,48]{1,0:T(8,128)} %north_hbm.1) | copy-start | bytes 27652

commit v3 on v2

--- a/solution.py
+++ b/solution.py
@@ -10,6 +10,7 @@
 from jax.sharding import PartitionSpec as P
 
 STEPS = 3
+CHUNK = 2
 MESH = pl.DeviceIdType.MESH
 
 
@@ -266,6 +267,7 @@
     rows_fine, band = east_in.shape
     halo = 2 * STEPS
     width = band + 2 * halo
+    chunks = [(i, min(i + CHUNK, members)) for i in range(0, members, CHUNK)]
 
     loads = []
     sources = (
@@ -288,7 +290,7 @@
             barrier, inc=1, device_id={"mem": lax.rem(m + d, mems)}, device_id_type=MESH
         )
 
-    def spread_out(kind, axis, source, target):
+    def spread_out(kind, axis, source, target, place=lambda ref, me: ref.at[me]):
         size, me = (tiles, t) if axis == "tile" else (mems, m)
         sends, recvs = (tile_send, tile_recv) if axis == "tile" else (mem_send, mem_recv)
         copies = []
@@ -296,7 +298,7 @@
             dest = lax.rem(me + d, size)
             copy = pltpu.make_async_remote_copy(
                 src_ref=source(dest),
-                dst_ref=target.at[me],
+                dst_ref=place(target, me),
                 send_sem=sends.at[kind, d],
                 recv_sem=recvs.at[kind, d],
                 device_id={axis: dest},
@@ -304,29 +306,40 @@
             )
             copy.start()
             copies.append(copy)
-        target[me] = source(me)[...]
+        place(target, me)[...] = source(me)[...]
         started.extend(copies)
         return copies
+
+    def exchange(kind, chunk, source, target):
+        low, high = chunks[chunk]
+        span = pl.ds(low, high - low)
+        return spread_out(
+            3 + kind * len(chunks) + chunk,
+            "tile",
+            lambda dest: source.at[dest, span],
+            target,
+            lambda ref, me: ref.at[me, span],
+        )
 
     def arrive(copies):
         for copy in copies:
             copy.wait_recv()
 
-    def store_pieces(target, value):
+    def store_pieces(target, value, low, high):
         for lane_part in range(-(-cols // 128)):
-            low = 128 * lane_part
-            span = min(128, cols - low)
+            at = 128 * lane_part
+            span = min(128, cols - at)
             for group in range(levels // 8):
                 piece = lane_part * (levels // 8) + group
-                block = value[:, 8 * group : 8 * group + 8, low : low + span]
-                target[piece] = wide(block) if span < 128 else block
-
-    def load_pieces(source):
+                block = value[:, 8 * group : 8 * group + 8, at : at + span]
+                target[piece, low:high] = wide(block) if span < 128 else block
+
+    def load_pieces(source, low, high):
         groups = levels // 8
         lanes = []
         for lane_part in range(-(-cols // 128)):
             span = min(128, cols - 128 * lane_part)
-            blocks = [source[lane_part * groups + g] for g in range(groups)]
+            blocks = [source[lane_part * groups + g, low:high] for g in range(groups)]
             lanes.append(jnp.concatenate(blocks, axis=1)[:, :, :span])
         return jnp.concatenate(lanes, axis=2)
 
@@ -336,14 +349,6 @@
     gain_row = rates[0:1, :]
     for r in range(1, rows):
         gain_row = gain_row * rates[r : r + 1, :]
-    loads[1].wait()
-    local_rows = []
-    state = None
-    for r in range(rows):
-        term = shrink[r] * ctl[:, r]
-        state = term if r == 0 else rate[r] * state + term
-        local_rows.append(state)
-    store_pieces(send_a, state)
     loads[2].wait()
     small[...] = jnp.zeros_like(small)
     small[0 : 2 * rows, :] = jnp.broadcast_to(
@@ -352,8 +357,20 @@
     small[2 * rows : 2 * rows + 1, :] = wide(gain_row)
 
     pl.semaphore_wait(barrier, tiles - 1 + mems - 1)
-    carry_copies = spread_out(1, "tile", lambda dest: send_a.at[dest], got_a)
     small_copies = spread_out(0, "tile", lambda dest: small, smalls)
+    loads[1].wait()
+    local_rows = []
+    carry_copies = []
+    for c, (low, high) in enumerate(chunks):
+        state = None
+        states = []
+        for r in range(rows):
+            term = shrink[r] * ctl[low:high, r]
+            state = term if r == 0 else rate[r] * state + term
+            states.append(state)
+        local_rows.append(states)
+        store_pieces(send_a, state, low, high)
+        carry_copies.append(exchange(0, c, send_a, got_a))
 
     for load in loads[3:]:
         load.wait()
@@ -391,10 +408,10 @@
     table = split(jnp.where(lane >= sub, math.sqrt(1.0 - LON_RATE**2) * powers, 0.0))
 
     def smooth(x, turned):
-        flat = x.reshape(members * levels, cols)
-        return product(split(flat), table, turned).reshape(members, levels, cols)
-
-    smooth_rows = [smooth(x, False) for x in local_rows]
+        flat = x.reshape(x.shape[0] * levels, cols)
+        return product(split(flat), table, turned).reshape(x.shape)
+
+    smooth_rows = [[smooth(x, False) for x in states] for states in local_rows]
 
     arrive(small_copies)
     group = lax.rem(t, levels // 8)
@@ -405,15 +422,17 @@
     for s in range(tiles):
         row = smalls[s, 2 * rows : 2 * rows + 1, :]
         gains.append(jnp.sum(jnp.where(gain_mask, row, 0.0), axis=1, keepdims=True))
-    arrive(carry_copies)
-    state = jnp.zeros((members, 8, 128), f32)
-    for s in range(tiles):
-        send_b[s] = state
-        state = gains[s] * state + got_a[s]
-    back_copies = spread_out(2, "tile", lambda dest: send_b.at[dest], got_b)
-
-    count = lon_in.shape[1]
-    lon_row = jnp.broadcast_to(lon_in[...].astype(f32) / 256.0, (8, count))
+    back_copies = []
+    for c, (low, high) in enumerate(chunks):
+        arrive(carry_copies[c])
+        state = jnp.zeros((high - low, 8, 128), f32)
+        for s in range(tiles):
+            send_b[s, low:high] = state
+            state = gains[s] * state + got_a[s, low:high]
+        back_copies.append(exchange(1, c, send_b, got_b))
+
+    count = lon_in.shape[0]
+    lon_row = jnp.broadcast_to(lon_in[...].astype(f32)[None] / 256.0, (8, count))
     slot = lax.broadcasted_iota(jnp.int32, (cols, 128), 0)
     lane = lax.broadcasted_iota(jnp.int32, (cols, 128), 1)
     for i in range(tiles):
@@ -440,15 +459,20 @@
         slabs.append(slab[None])
     weights[...] = jnp.swapaxes(jnp.concatenate(slabs, axis=0), 0, 1)
 
-    arrive(back_copies)
-    carried = smooth(load_pieces(got_b), False)
-    gain = None
+    partial = [jnp.zeros((levels, cols), f32)] * rows
+    for c, (low, high) in enumerate(chunks):
+        arrive(back_copies[c])
+        carried = smooth(load_pieces(got_b, low, high), False)
+        gain = None
+        for r in range(rows):
+            gain = rate[r] if r == 0 else gain * rate[r]
+            localized = gain * carried + smooth_rows[c][r]
+            partial[r] = partial[r] + jnp.sum(prt[low:high, r].astype(f32) * localized, axis=0)
     for r in range(rows):
-        gain = rate[r] if r == 0 else gain * rate[r]
-        localized = gain * carried + smooth_rows[r]
-        partial = spread * jnp.sum(prt[:, r].astype(f32) * localized, axis=0)
         for i in range(mems):
-            parts[i, 8 * r : 8 * r + 8] = partial[i * group_levels : (i + 1) * group_levels]
+            parts[i, 8 * r : 8 * r + 8] = (
+                spread * partial[r][i * group_levels : (i + 1) * group_levels]
+            )
     part_copies = spread_out(0, "mem", lambda dest: parts.at[dest], parts_got)
     east = expand(wind_rows.at[0], rows_fine)
     north = expand(wind_rows.at[1], rows_fine)
@@ -465,7 +489,7 @@
     every = product(split(total), (interp[...],), False)
     for i in range(tiles):
         rows_out[i] = every[:, 128 * i : 128 * (i + 1)]
-    row_copies = spread_out(3, "tile", lambda dest: rows_out.at[dest], rows_in)
+    row_copies = spread_out(1, "tile", lambda dest: rows_out.at[dest], rows_in)
     arrive(row_copies)
 
     coarse = tiles * rows
@@ -511,37 +535,49 @@
     g = jnp.where((lane >= halo) & (lane < halo + band), g, 0.0)
     adjoint = paired(lat * g) + southward(paired((1.0 - lat) * g))
     adj_out[...] = adjoint.reshape(tiles, rows * 8, 128)
-    adj_copies = spread_out(4, "tile", lambda dest: adj_out.at[dest], adj_in)
+    adj_copies = spread_out(2, "tile", lambda dest: adj_out.at[dest], adj_in)
     arrive(adj_copies)
     every = jnp.concatenate([adj_in[i] for i in range(tiles)], axis=1)
     own_adj[...] = product(split(every), (interp[...],), True)
     own_copies = spread_out(1, "mem", lambda dest: own_adj, adj_all)
     arrive(own_copies)
 
-    member_rows = []
+    fields = []
     for r in range(rows):
         field = jnp.concatenate([adj_all[i, 8 * r : 8 * r + 8] for i in range(mems)], axis=0)
-        member_rows.append((spread * field) * prt[:, r].astype(f32))
-    state = member_rows[rows - 1]
-    summed = [state]
-    for r in reversed(range(rows - 1)):
-        state = member_rows[r] + rate[r + 1] * state
-        summed.insert(0, state)
-    store_pieces(send_c, rate[0] * state)
-    up_copies = spread_out(5, "tile", lambda dest: send_c.at[dest], got_c)
-    smooth_rows = [smooth(shrink[r] * summed[r], True) for r in range(rows)]
-    arrive(up_copies)
-    state = jnp.zeros((members, 8, 128), f32)
-    for s in reversed(range(tiles)):
-        send_d[s] = state
-        state = gains[s] * state + got_c[s]
-    last_copies = spread_out(6, "tile", lambda dest: send_d.at[dest], got_d)
-    arrive(last_copies)
-    carried = smooth(load_pieces(got_d), True)
-    gain = None
-    for r in reversed(range(rows)):
-        gain = jnp.ones_like(rate[r]) if r == rows - 1 else gain * rate[r + 1]
-        out[:, r] = ctl[:, r] + smooth_rows[r] + (shrink[r] * gain) * carried
+        fields.append(spread * field)
+    summed = []
+    up_copies = []
+    for c, (low, high) in enumerate(chunks):
+        state = None
+        states = []
+        for r in reversed(range(rows)):
+            term = fields[r] * prt[low:high, r].astype(f32)
+            state = term if r == rows - 1 else term + rate[r + 1] * state
+            states.insert(0, state)
+        summed.append(states)
+        store_pieces(send_c, rate[0] * state, low, high)
+        up_copies.append(exchange(2, c, send_c, got_c))
+    smooth_rows = [
+        [smooth(shrink[r] * states[r], True) for r in range(rows)] for states in summed
+    ]
+    last_copies = []
+    for c, (low, high) in enumerate(chunks):
+        arrive(up_copies[c])
+        state = jnp.zeros((high - low, 8, 128), f32)
+        for s in reversed(range(tiles)):
+            send_d[s, low:high] = state
+            state = gains[s] * state + got_c[s, low:high]
+        last_copies.append(exchange(3, c, send_d, got_d))
+    for c, (low, high) in enumerate(chunks):
+        arrive(last_copies[c])
+        carried = smooth(load_pieces(got_d, low, high), True)
+        gain = None
+        for r in reversed(range(rows)):
+            gain = jnp.ones_like(rate[r]) if r == rows - 1 else gain * rate[r + 1]
+            out[low:high, r] = (
+                ctl[low:high, r] + smooth_rows[c][r] + (shrink[r] * gain) * carried
+            )
     for copy in started:
         copy.wait_send()
 
@@ -557,20 +593,21 @@
     prt = jnp.transpose(perturbations, (0, 2, 1, 3))
     group = levels // mems
     spread = float(1.0 / np.sqrt(np.float32(members * mems - 1)))
+    kinds = 3 + 4 * -(-members // CHUNK)
     piece = pltpu.VMEM((tiles, members, 8, 128), f32)
     partial = pltpu.VMEM((mems, rows * group, cols), f32)
     window = pltpu.VMEM((tiles, rows * group, 128), f32)
     result = pl.pallas_call(
         functools.partial(hessian_kernel, tiles, mems, spread),
         out_shape=jax.ShapeDtypeStruct(ctl.shape, f32),
-        in_specs=[pl.BlockSpec(memory_space=pl.ANY)] * 8,
+        in_specs=[pl.BlockSpec(memory_space=pltpu.HBM)] * 8,
         out_specs=pl.BlockSpec(memory_space=pltpu.VMEM),
         scratch_shapes=[
             pltpu.VMEM(ctl.shape, f32),
             pltpu.VMEM(prt.shape, prt.dtype),
             pltpu.VMEM(filter_rate.shape, f32),
             pltpu.VMEM((1, lat_weight.shape[0]), i32),
-            pltpu.VMEM((1, lon_weight.shape[0]), i32),
+            pltpu.VMEM(lon_weight.shape, i32),
             pltpu.VMEM((rows_fine, band), i32),
             pltpu.VMEM((rows_fine, band), i32),
             pltpu.VMEM((group, rows_fine, band), f32),
@@ -590,16 +627,16 @@
             pltpu.SemaphoreType.DMA((8,)),
             pltpu.SemaphoreType.DMA((2,)),
             pltpu.SemaphoreType.DMA((2,)),
-            pltpu.SemaphoreType.DMA((7, tiles)),
-            pltpu.SemaphoreType.DMA((7, tiles)),
+            pltpu.SemaphoreType.DMA((kinds, tiles)),
+            pltpu.SemaphoreType.DMA((kinds, tiles)),
             pltpu.SemaphoreType.DMA((2, mems)),
             pltpu.SemaphoreType.DMA((2, mems)),
         ],
         compiler_params=pltpu.CompilerParams(
-            collective_id=0, has_side_effects=True, vmem_limit_bytes=40 * 2**20
+            collective_id=0, has_side_effects=True, vmem_limit_bytes=60 * 2**20
         ),
     )(
-        ctl, prt, filter_rate, lat_weight[None], lon_weight[None], wind_east, wind_north,
+        ctl, prt, filter_rate, lat_weight[None], lon_weight, wind_east, wind_north,
         obs_weight,
     )
     return jnp.transpose(result, (0, 2, 1, 3))

time: 52.3 us -> 47.9 us (0.916)
  local copies, waits for them, and re-layouts: 6.72 us -> 1.85 us
  Pallas kernels: 45.2 us -> 45.9 us
    unnamed x17 -> x1, local copies, waits for them, and re-layouts: 6.72 us -> 1.85 us
    pallas_call x1, Pallas kernels: 45.2 us -> 45.9 us  [fused(): pl.pallas_call(functools.partial(hessian_kernel, tiles, mems, spread), ou...]
where the time goes in v3:
time: 47.9 us; the launch traced here: 47.7 us
  Pallas kernels  45.9 us (96%)
  local copies, waits for them, and re-layouts  1.85 us (4%)
    pallas_call x1, Pallas kernels, fused(): pl.pallas_call(functools.partial(hessian_kernel, tiles, mems, spread), ou...  45.9 us
    unnamed x1, local copies, waits for them, and re-layouts  1.85 us

profile of v3, /device:TPU:0, one launch (start us, length us, event | category | flops | bytes accessed | tf_op | source)
XLA Modules:
  0.0 47.7 jit_solution(16292890563287005914)
XLA Ops:
  0.0 45.9 %shard_map.82 = f32[5,3,32,192]{3,2,1,0:T(8,128)} custom-call(f32[5,3,32,192]{3,2,1,0:T(8,128)} %bitcast.5, bf16[5,3,32,192]{3,2,1,0:T(8,128)(2,1)} %bitcast.6, f32[3,32]{1,0:T(4,128)} %rates_hbm.1, s32[1,6]{1,0:T(1,128)} %bitcast.7, s32[384]{0:T(512)} %lon_hbm.1, s32[48,48]{1,0:T(8,128)} %east_hbm.1, s32[48,48]{1,0:T(8,128)} %north_hbm.1, f32[32,48,48]{2,1,0:T(8,128)} %obs_hbm.1), custom_call_target="tpu_custom_call" | custom-call | tf_op jit(solution)/shard_map/pallas_call | solution.py:600
  45.9 1.9 %copy.10 = f32[5,32,3,192]{3,1,2,0:T(8,128)} copy(f32[5,32,3,192]{3,1,2,0:T(8,128)} %bitcast.4) | data formatting | bytes 737280

commit v4 on v3

--- a/solution.py
+++ b/solution.py
@@ -267,7 +267,10 @@
     rows_fine, band = east_in.shape
     halo = 2 * STEPS
     width = band + 2 * halo
-    chunks = [(i, min(i + CHUNK, members)) for i in range(0, members, CHUNK)]
+    slots = send_a.shape[1]
+    chunks = [(i, min(i + CHUNK, slots)) for i in range(0, slots, CHUNK)]
+    ends = [min(members, 256 * high // cols) for low, high in chunks[:-1]] + [members]
+    sets = list(zip([0] + ends[:-1], ends))
 
     loads = []
     sources = (
@@ -325,23 +328,43 @@
         for copy in copies:
             copy.wait_recv()
 
-    def store_pieces(target, value, low, high):
-        for lane_part in range(-(-cols // 128)):
-            at = 128 * lane_part
-            span = min(128, cols - at)
-            for group in range(levels // 8):
-                piece = lane_part * (levels // 8) + group
-                block = value[:, 8 * group : 8 * group + 8, at : at + span]
-                target[piece, low:high] = wide(block) if span < 128 else block
+    groups = levels // 8
+    half = cols // 2
+
+    def store_pieces(target, value):
+        for side in range(2):
+            lanes = [x[:, side * half : (side + 1) * half] for x in value]
+            spare = slots * 128 - members * half
+            if spare:
+                lanes.append(jnp.zeros((levels, spare), f32))
+            row = jnp.concatenate(lanes, axis=1)
+            for group in range(groups):
+                for k in range(slots):
+                    target[side * groups + group, k] = row[
+                        8 * group : 8 * group + 8, 128 * k : 128 * k + 128
+                    ]
 
     def load_pieces(source, low, high):
-        groups = levels // 8
-        lanes = []
-        for lane_part in range(-(-cols // 128)):
-            span = min(128, cols - 128 * lane_part)
-            blocks = [source[lane_part * groups + g, low:high] for g in range(groups)]
-            lanes.append(jnp.concatenate(blocks, axis=1)[:, :, :span])
-        return jnp.concatenate(lanes, axis=2)
+        first, last = low * half // 128, -(-high * half // 128)
+        sides = []
+        for side in range(2):
+            row = jnp.concatenate(
+                [
+                    jnp.concatenate(
+                        [source[side * groups + g, k] for g in range(groups)], axis=0
+                    )
+                    for k in range(first, last)
+                ],
+                axis=1,
+            )
+            sides.append(row)
+        value = []
+        for i in range(low, high):
+            at = i * half - 128 * first
+            value.append(
+                jnp.concatenate([row[:, at : at + half] for row in sides], axis=1)[None]
+            )
+        return jnp.concatenate(value, axis=0)
 
     loads[0].wait()
     rate = [column(rates[r : r + 1, :]) for r in range(rows)]
@@ -360,17 +383,13 @@
     small_copies = spread_out(0, "tile", lambda dest: small, smalls)
     loads[1].wait()
     local_rows = []
-    carry_copies = []
-    for c, (low, high) in enumerate(chunks):
-        state = None
-        states = []
-        for r in range(rows):
-            term = shrink[r] * ctl[low:high, r]
-            state = term if r == 0 else rate[r] * state + term
-            states.append(state)
-        local_rows.append(states)
-        store_pieces(send_a, state, low, high)
-        carry_copies.append(exchange(0, c, send_a, got_a))
+    state = None
+    for r in range(rows):
+        term = shrink[r] * ctl[:, r]
+        state = term if r == 0 else rate[r] * state + term
+        local_rows.append(state)
+    store_pieces(send_a, [state[i] for i in range(members)])
+    carry_copies = [exchange(0, c, send_a, got_a) for c in range(len(chunks))]
 
     for load in loads[3:]:
         load.wait()
@@ -411,7 +430,7 @@
         flat = x.reshape(x.shape[0] * levels, cols)
         return product(split(flat), table, turned).reshape(x.shape)
 
-    smooth_rows = [[smooth(x, False) for x in states] for states in local_rows]
+    smooth_rows = [smooth(x, False) for x in local_rows]
 
     arrive(small_copies)
     group = lax.rem(t, levels // 8)
@@ -460,13 +479,13 @@
     weights[...] = jnp.swapaxes(jnp.concatenate(slabs, axis=0), 0, 1)
 
     partial = [jnp.zeros((levels, cols), f32)] * rows
-    for c, (low, high) in enumerate(chunks):
+    for c, (low, high) in enumerate(sets):
         arrive(back_copies[c])
         carried = smooth(load_pieces(got_b, low, high), False)
         gain = None
         for r in range(rows):
             gain = rate[r] if r == 0 else gain * rate[r]
-            localized = gain * carried + smooth_rows[c][r]
+            localized = gain * carried + smooth_rows[r][low:high]
             partial[r] = partial[r] + jnp.sum(prt[low:high, r].astype(f32) * localized, axis=0)
     for r in range(rows):
         for i in range(mems):
@@ -488,7 +507,12 @@
         total = total + parts_got[i]
     every = product(split(total), (interp[...],), False)
     for i in range(tiles):
-        rows_out[i] = every[:, 128 * i : 128 * (i + 1)]
+        for r in range(0, rows, 2):
+            block = every[8 * r : 8 * r + 8, 128 * i : 128 * (i + 1)]
+            if r + 1 < rows:
+                other = every[8 * r + 8 : 8 * r + 16, 128 * i : 128 * (i + 1)]
+                block = block + pltpu.roll(other, 64, 1)
+            rows_out[i, 4 * r : 4 * r + 8] = block
     row_copies = spread_out(1, "tile", lambda dest: rows_out.at[dest], rows_in)
     arrive(row_copies)
 
@@ -512,7 +536,13 @@
         flat = x.reshape(rows_fine * 8, 128)
         return pltpu.roll(flat, distance, 1).reshape(rows_fine, 8, 128)
 
-    increment = rows_in[...].reshape(coarse, 8, 128)
+    def unpacked(ref, i, r):
+        block = ref[i, 8 * (r // 2) : 8 * (r // 2) + 8]
+        return pltpu.roll(block, 64, 1) if r % 2 else block
+
+    increment = jnp.concatenate(
+        [unpacked(rows_in, i, r)[None] for i in range(tiles) for r in range(rows)], axis=0
+    )
     g = lat * doubled(increment) + (1.0 - lat) * doubled(northward(increment))
     for _ in range(STEPS):
         g = (
@@ -534,10 +564,21 @@
     lane = lax.broadcasted_iota(jnp.int32, g.shape, 2)
     g = jnp.where((lane >= halo) & (lane < halo + band), g, 0.0)
     adjoint = paired(lat * g) + southward(paired((1.0 - lat) * g))
-    adj_out[...] = adjoint.reshape(tiles, rows * 8, 128)
+    for i in range(tiles):
+        for r in range(0, rows, 2):
+            block = adjoint[i * rows + r]
+            if r + 1 < rows:
+                block = block + pltpu.roll(adjoint[i * rows + r + 1], 64, 1)
+            adj_out[i, 4 * r : 4 * r + 8] = block
     adj_copies = spread_out(2, "tile", lambda dest: adj_out.at[dest], adj_in)
     arrive(adj_copies)
-    every = jnp.concatenate([adj_in[i] for i in range(tiles)], axis=1)
+    every = jnp.concatenate(
+        [
+            jnp.concatenate([unpacked(adj_in, i, r) for i in range(tiles)], axis=1)
+            for r in range(rows)
+        ],
+        axis=0,
+    )
     own_adj[...] = product(split(every), (interp[...],), True)
     own_copies = spread_out(1, "mem", lambda dest: own_adj, adj_all)
     arrive(own_copies)
@@ -547,20 +588,15 @@
         field = jnp.concatenate([adj_all[i, 8 * r : 8 * r + 8] for i in range(mems)], axis=0)
         fields.append(spread * field)
     summed = []
-    up_copies = []
-    for c, (low, high) in enumerate(chunks):
-        state = None
-        states = []
-        for r in reversed(range(rows)):
-            term = fields[r] * prt[low:high, r].astype(f32)
-            state = term if r == rows - 1 else term + rate[r + 1] * state
-            states.insert(0, state)
-        summed.append(states)
-        store_pieces(send_c, rate[0] * state, low, high)
-        up_copies.append(exchange(2, c, send_c, got_c))
-    smooth_rows = [
-        [smooth(shrink[r] * states[r], True) for r in range(rows)] for states in summed
-    ]
+    state = None
+    for r in reversed(range(rows)):
+        term = fields[r] * prt[:, r].astype(f32)
+        state = term if r == rows - 1 else term + rate[r + 1] * state
+        summed.insert(0, state)
+    carry = rate[0] * state
+    store_pieces(send_c, [carry[i] for i in range(members)])
+    up_copies = [exchange(2, c, send_c, got_c) for c in range(len(chunks))]
+    smooth_rows = [smooth(shrink[r] * summed[r], True) for r in range(rows)]
     last_copies = []
     for c, (low, high) in enumerate(chunks):
         arrive(up_copies[c])
@@ -569,15 +605,13 @@
             send_d[s, low:high] = state
             state = gains[s] * state + got_c[s, low:high]
         last_copies.append(exchange(3, c, send_d, got_d))
-    for c, (low, high) in enumerate(chunks):
+    for c, (low, high) in enumerate(sets):
         arrive(last_copies[c])
         carried = smooth(load_pieces(got_d, low, high), True)
         gain = None
         for r in reversed(range(rows)):
             gain = jnp.ones_like(rate[r]) if r == rows - 1 else gain * rate[r + 1]
-            out[low:high, r] = (
-                ctl[low:high, r] + smooth_rows[c][r] + (shrink[r] * gain) * carried
-            )
+            out[low:high, r] = smooth_rows[r][low:high] + (shrink[r] * gain) * carried
     for copy in started:
         copy.wait_send()
 
@@ -593,10 +627,11 @@
     prt = jnp.transpose(perturbations, (0, 2, 1, 3))
     group = levels // mems
     spread = float(1.0 / np.sqrt(np.float32(members * mems - 1)))
-    kinds = 3 + 4 * -(-members // CHUNK)
-    piece = pltpu.VMEM((tiles, members, 8, 128), f32)
+    slots = -(-members * (cols // 2) // 128)
+    kinds = 3 + 4 * -(-slots // CHUNK)
+    piece = pltpu.VMEM((tiles, slots, 8, 128), f32)
     partial = pltpu.VMEM((mems, rows * group, cols), f32)
-    window = pltpu.VMEM((tiles, rows * group, 128), f32)
+    window = pltpu.VMEM((tiles, -(-rows // 2) * group, 128), f32)
     result = pl.pallas_call(
         functools.partial(hessian_kernel, tiles, mems, spread),
         out_shape=jax.ShapeDtypeStruct(ctl.shape, f32),
@@ -639,7 +674,7 @@
         ctl, prt, filter_rate, lat_weight[None], lon_weight, wind_east, wind_north,
         obs_weight,
     )
-    return jnp.transpose(result, (0, 2, 1, 3))
+    return control + jnp.transpose(result, (0, 2, 1, 3))
 
 
 def plan(
@@ -650,12 +685,13 @@
     rows_fine, band = wind_east.shape
     fits = (
         levels == 8 * mems
-        and levels // 8 * -(-cols // 128) == tiles
+        and levels // 8 * 2 == tiles
+        and cols % 2 == 0
         and tiles > 2
         and 2 * rows + 1 <= 8
         and rows_fine == 2 * rows * tiles
         and rows_fine % 8 == 0
-        and 2 * STEPS <= band <= 128 - 4 * STEPS
+        and 2 * STEPS <= band <= 64 - 4 * STEPS
         and levels <= 128
     )
     return (fused if fits else local)(

time: 47.9 us -> 45.1 us (0.942)
  Pallas kernels: 45.9 us -> 43.1 us
  other arithmetic: 0 us -> 1.88 us
  local copies, waits for them, and re-layouts: 1.85 us -> 0.01 us
    pallas_call x1, Pallas kernels: 45.9 us -> 43.1 us  [fused(): pl.pallas_call(functools.partial(hessian_kernel, tiles, mems, spread), ou...]
    add x0 -> x1, other arithmetic: none -> 1.88 us  [fused(): return control + jnp.transpose(result, (0, 2, 1, 3))]
    unnamed x1 -> x2, local copies, waits for them, and re-layouts: 1.85 us -> 0.01 us
where the time goes in v4:
time: 45.1 us; the launch traced here: 45 us
  Pallas kernels  43.1 us (96%)
  other arithmetic  1.88 us (4%)
    pallas_call x1, Pallas kernels, fused(): pl.pallas_call(functools.partial(hessian_kernel, tiles, mems, spread), ou...  43.1 us
    add x1, other arithmetic, fused(): return control + jnp.transpose(result, (0, 2, 1, 3))  1.88 us

profile of v4, /device:TPU:0, one launch (start us, length us, event | category | flops | bytes accessed | tf_op | source)
XLA Modules:
  0.0 45.0 jit_solution(1729187363111194620)
XLA Ops:
  0.0 0.0 copy-start
  0.0 43.1 %shard_map.82 = f32[5,3,32,192]{3,2,1,0:T(8,128)} custom-call(f32[5,3,32,192]{3,2,1,0:T(8,128)} %bitcast.5, bf16[5,3,32,192]{3,2,1,0:T(8,128)(2,1)} %bitcast.6, f32[3,32]{1,0:T(4,128)} %rates_hbm.1, s32[1,6]{1,0:T(1,128)} %bitcast.7, s32[384]{0:T(512)} %lon_hbm.1, s32[48,48]{1,0:T(8,128)} %east_hbm.1, s32[48,48]{1,0:T(8,128)} %north_hbm.1, f32[32,48,48]{2,1,0:T(8,128)} %obs_hbm.1), custom_call_target="tpu_custom_call" | custom-call | tf_op jit(solution)/shard_map/pallas_call | solution.py:635
  43.1 0.0 copy-done
  43.1 1.9 %bitcast_add_fusion = f32[5,32,3,192]{3,1,2,0:T(8,128)} fusion(f32[5,32,3,192]{3,1,2,0:T(8,128)S(1)} %copy-done, f32[5,3,32,192]{3,2,1,0:T(8,128)} %shard_map.82), kind=kLoop, calls=%fused_computation | loop fusion | flops 92160 | bytes 1105920 | tf_op jit(solution)/shard_map/add | solution.py:677
Async XLA Ops:
  0.0 43.1 %copy-start = (f32[5,32,3,192]{3,1,2,0:T(8,128)S(1)}, f32[5,32,3,192]{3,1,2,0:T(8,128)}, u32[]{:S(2)}) copy-start(f32[5,32,3,192]{3,1,2,0:T(8,128)} %param.9) | copy-start | bytes 1105924
